TPU v7x, 32 devices: a whole 2x2x4 slice. The times are simulated.
32 devices in a mesh: slab: 8 (over y, x, core), sub: 4 (over z).
Axes of the slice: x: 2, y: 2, z: 4, core: 2. Of those that a mesh axis runs over, the one named last changes fastest.
Arguments:
- field_init: float32 [3, 64, 64, 128], P(None, 'slab', 'sub'), may hold values from -6 to 6
- load: float32 [3, 64, 64, 128], P(None, 'slab', 'sub'), may hold values from -6 to 6
- modulus: float32 [64, 64, 128], P('slab', 'sub'), may hold values from 0.3 to 3
- seg_z: int32 [64], P('slab'), may hold values from 0 to 15, as said below
- seg_y: int32 [64], P('sub'), may hold values from 0 to 15, as said below
- seg_x: int32 [128], replicated, may hold values from 0 to 31, as said below
Outputs:
- smoothed: float32 [3, 64, 64, 128], P(None, 'slab', 'sub')
- coarse: float32 [6, 16, 512], P(None, 'slab', 'sub')
Inputs may be any that keep to these rules, and one draw needn't show every extreme that they name: `seg_z`: along z, segment k starts at node 4 k or 4 k + 1 (segment 0 at 0, the last segment at 4 k + 1) and runs to the next start or the grid's end; entries never fall. `seg_y`: along y, segment k starts at node 4 k or 4 k + 1 (segment 0 at 0, the last segment at 4 k + 1) and runs to the next start or the grid's end; entries never fall. `seg_x`: along x, segment k starts at node 4 k or 4 k + 1 (segment 0 at 0, the last segment at 4 k + 1) and runs to the next start or the grid's end; entries never fall.
All inputs are finite; a program needn't handle non-finite values.
Results may differ from a plain program's by a relative error of at most 0.0003.
Values sent between devices are 32-bit elements; how exact they have to be, the bound alone decides.
A program may use at most 64 MiB of HBM per device.

v0:
```python
import functools

import jax
import jax.numpy as jnp
from jax import lax
from jax.experimental import pallas as pl
from jax.experimental.pallas import tpu as pltpu
from jax.sharding import PartitionSpec as P

SWEEPS = 2
DAMPING = 0.6
LOW = SWEEPS + 1
HIGH = SWEEPS + 2
REACH = ((LOW, HIGH), (LOW - 1, HIGH - 1), (LOW, HIGH - 1))
POISSON = 0.3
LAME = POISSON / ((1.0 + POISSON) * (1.0 - 2.0 * POISSON))
SHEAR = 0.5 / (1.0 + POISSON)
SIDES = [(dz, dy) for dz in (-1, 1, 0) for dy in (0, -1, 1) if (dz, dy) != (0, 0)]
MESH = pl.DeviceIdType.MESH
F32 = jnp.float32


def spans(step, size, reach):
    low, high = reach
    if step == 1:
        return (size - low, LOW - low, low)
    if step == -1:
        return (0, LOW + size, high)
    return (0, LOW, size)


def halo_kernel(field, load, mod, seg_z, seg_y, ext, mark, send_sem, recv_sem, own_sem):
    size_z, size_y = mod.shape[0], mod.shape[1]
    slab, sub = lax.axis_index("slab"), lax.axis_index("sub")
    slabs, subs = lax.axis_size("slab"), lax.axis_size("sub")

    def present(dz, dy):
        there = jnp.bool_(True)
        if dz == 1:
            there = there & (slab < slabs - 1)
        if dz == -1:
            there = there & (slab > 0)
        if dy == 1:
            there = there & (sub < subs - 1)
        if dy == -1:
            there = there & (sub > 0)
        return there

    barrier = pltpu.get_barrier_semaphore()
    for dz, dy in SIDES:

        @pl.when(present(dz, dy))
        def _():
            pl.semaphore_signal(
                barrier, inc=1, device_id=(slab + dz, sub + dy), device_id_type=MESH
            )

    own = [
        pltpu.make_async_copy(
            src, ext.at[pl.ds(3 * k, 3), pl.ds(LOW, size_z), pl.ds(LOW, size_y)], own_sem.at[k]
        )
        for k, src in enumerate((field, load))
    ]
    own.append(
        pltpu.make_async_copy(
            mod, ext.at[6, pl.ds(LOW, size_z), pl.ds(LOW, size_y)], own_sem.at[2]
        )
    )
    for copy in own:
        copy.start()
    mark[0] = jnp.full((1, mark.shape[-1]), seg_z[0].astype(F32))
    mark[1] = jnp.full((1, mark.shape[-1]), seg_y[0].astype(F32))
    peers_z = 3 - (slab == 0).astype(jnp.int32) - (slab == slabs - 1).astype(jnp.int32)
    peers_y = 3 - (sub == 0).astype(jnp.int32) - (sub == subs - 1).astype(jnp.int32)
    pl.semaphore_wait(barrier, peers_z * peers_y - 1)

    copies = []
    for side, (dz, dy) in enumerate(SIDES):
        there = (slab + dz, sub + dy)
        group = []
        for k, src in enumerate((field, load, mod)):
            sz, tz, nz = spans(dz, size_z, REACH[k])
            sy, ty, ny = spans(dy, size_y, REACH[k])
            if k < 2:
                from_ref = src.at[:, pl.ds(sz, nz), pl.ds(sy, ny)]
                to_ref = ext.at[pl.ds(3 * k, 3), pl.ds(tz, nz), pl.ds(ty, ny)]
            else:
                from_ref = src.at[pl.ds(sz, nz), pl.ds(sy, ny)]
                to_ref = ext.at[6, pl.ds(tz, nz), pl.ds(ty, ny)]
            group.append((from_ref, to_ref, k))
        if (dz, dy) == (-1, 0):
            group.append((mark.at[0], ext.at[6, ext.shape[1] - 1, 0], 3))
        if (dz, dy) == (0, -1):
            group.append((mark.at[1], ext.at[6, ext.shape[1] - 1, 1], 3))
        group = [
            pltpu.make_async_remote_copy(
                src_ref=from_ref,
                dst_ref=to_ref,
                send_sem=send_sem.at[side, k],
                recv_sem=recv_sem.at[side, k],
                device_id=there,
                device_id_type=MESH,
            )
            for from_ref, to_ref, k in group
        ]
        copies.append(group)

        @pl.when(present(dz, dy))
        def _():
            for copy in group:
                copy.start()

    for copy in own:
        copy.wait()
    for (dz, dy), group in zip(SIDES, copies):

        @pl.when(present(dz, dy))
        def _():
            for copy in group:
                copy.wait_send()

        @pl.when(present(-dz, -dy))
        def _():
            for copy in group:
                copy.wait_recv()


def element_modes(lo, hi, e):
    def up(c, x, y):
        return lo[c][x][y] + hi[c][x][y]

    def diff(c, x, y):
        return hi[c][x][y] - lo[c][x][y]

    e_shear = e * (SHEAR / 16.0)
    e_shear2 = e * (SHEAR / 8.0)
    e_lame = e * (LAME / 16.0)
    e_lame3 = e * (LAME / 48.0)
    e_shear3 = e * (SHEAR / 48.0)
    e_last = e * ((LAME + 4.0 * SHEAR) / 144.0)
    out = [[[[None, None], [None, None]] for _ in range(2)] for _ in range(3)]

    n0, n1, n2 = up(0, 1, 0), up(1, 0, 1), diff(2, 0, 0)
    both = e_lame * (n0 + n1 + n2)
    out[0][1][0][0] = both + e_shear2 * n0
    out[1][0][1][0] = both + e_shear2 * n1
    out[2][0][0][1] = both + e_shear2 * n2

    both = e_shear * (up(0, 0, 1) + up(1, 1, 0))
    out[0][0][1][0] = both
    out[1][1][0][0] = both
    both = e_shear * (diff(0, 0, 0) + up(2, 1, 0))
    out[0][0][0][1] = both
    out[2][1][0][0] = both
    both = e_shear * (diff(1, 0, 0) + up(2, 0, 1))
    out[1][0][0][1] = both
    out[2][0][1][0] = both

    a, b = up(0, 1, 1), diff(2, 0, 1)
    both = e_lame3 * (a + b)
    out[0][1][1][0] = both + e_shear * a
    out[2][0][1][1] = both + e_shear * b
    a, b = diff(0, 1, 0), diff(1, 0, 1)
    both = e_lame3 * (a + b)
    out[0][1][0][1] = both + e_shear * a
    out[1][0][1][1] = both + e_shear * b
    a, b = up(1, 1, 1), diff(2, 1, 0)
    both = e_lame3 * (a + b)
    out[1][1][1][0] = both + e_shear * a
    out[2][1][0][1] = both + e_shear * b

    a, b, c = diff(0, 0, 1), diff(1, 1, 0), up(2, 1, 1)
    both = a + b + c
    out[0][0][1][1] = e_shear3 * (both + a)
    out[1][1][0][1] = e_shear3 * (both + b)
    out[2][1][1][0] = e_shear3 * (both + c)

    for c in range(3):
        out[c][1][1][1] = e_last * diff(c, 1, 1)
    return out


def compute_kernel(
    seg_z, seg_y, seg_x, ext, smooth, coarse, cur, emod, inverse, modes, back, resid, *, unroll
):
    size_z, size_y, width = smooth.shape[1:]
    planes, rows = ext.shape[1], ext.shape[2]
    slab, sub = lax.axis_index("slab"), lax.axis_index("sub")
    total_z = size_z * lax.axis_size("slab")
    total_y = size_y * lax.axis_size("sub")
    first_z = slab * size_z - LOW
    first_y = sub * size_y - LOW
    row = lax.broadcasted_iota(jnp.int32, (rows, width), 0)
    column = lax.broadcasted_iota(jnp.int32, (rows, width), 1)
    glob_y = row + first_y
    rows_in = (glob_y >= 0) & (glob_y < total_y)
    last_row = LOW + size_y + HIGH - 1
    field_in = rows_in & (row <= last_row)
    load_in = rows_in & (row >= 1) & (row < last_row)
    elements_in = rows_in & (glob_y < total_y - 1) & (row < last_row) & (column < width - 1)

    def left(v):
        return pltpu.roll(v, v.shape[1] - 1, 1)

    def right(v):
        return pltpu.roll(v, 1, 1)

    def lower(v):
        return pltpu.roll(v, v.shape[0] - 1, 0)

    def upper(v):
        return pltpu.roll(v, 1, 0)

    def stage(q, _):
        glob_z = q + first_z
        plane_in = (glob_z >= 0) & (glob_z < total_z)
        for c in range(3):
            cur[c, q] = jnp.where(field_in & plane_in, ext[c, q], 0.0)
        inner = plane_in & (glob_z < total_z - 1) & (q < planes - 1)
        emod[q] = jnp.where(elements_in & inner, ext[6, q], 0.0)
        return 0

    lax.fori_loop(0, planes, stage, 0)

    def sum_modes(q):
        e = emod[q]
        r = right(e)
        s, d = e + r, r - e
        us, ud = upper(s), upper(d)
        return s + us, us - s, d + ud, ud - d

    def invert(q, before):
        now = sum_modes(q)
        main = (LAME + 4.0 * SHEAR) / 9.0
        side = (LAME + SHEAR) / 12.0
        p = main * (now[0] + before[0])
        xy = side * (now[3] + before[3])
        xz = side * (before[2] - now[2])
        yz = side * (before[1] - now[1])
        pp = p * p
        c00 = pp - yz * yz
        c11 = pp - xz * xz
        c22 = pp - xy * xy
        c01 = xz * yz - xy * p
        c02 = xy * yz - xz * p
        c12 = xy * xz - yz * p
        det = p * c00 + xy * c01 + xz * c02
        scale = DAMPING / jnp.where(p > 0.0, det, 1.0)
        for k, entry in enumerate((c00, c11, c22, c01, c02, c12)):
            inverse[k, q] = entry * scale
        return now

    lax.fori_loop(1, planes - 1, invert, sum_modes(0))

    def forward(q, _):
        for c in range(3):
            u = cur[c, q]
            a = left(u)
            for x, t in enumerate((u + a, a - u)):
                b = lower(t)
                modes[4 * c + 2 * x, q] = t + b
                modes[4 * c + 2 * x + 1, q] = b - t
        return 0

    def apply(first, last, finish):
        lax.fori_loop(first - 1, last + 1, forward, 0)
        for tile in range(rows // 8):
            at = pl.ds(8 * tile, 8)

            def element(q, carry):
                lo = [
                    [[modes[4 * c + 2 * x + y, q, at] for y in range(2)] for x in range(2)]
                    for c in range(3)
                ]
                hi = [
                    [[modes[4 * c + 2 * x + y, q + 1, at] for y in range(2)] for x in range(2)]
                    for c in range(3)
                ]
                out = element_modes(lo, hi, emod[q, at])
                after = []
                for c in range(3):
                    for x in range(2):
                        for y in range(2):
                            k = 4 * c + 2 * x + y
                            total, change = out[c][x][y]
                            if total is None:
                                back[k, q, at] = carry[k] - change
                                after.append(change)
                            else:
                                back[k, q, at] = carry[k] + (total - change)
                                after.append(total + change)
                return tuple(after)

            zero = jnp.zeros((8, width), F32)
            carry = element(first - 1, (zero,) * 12)
            lax.fori_loop(first, last, element, carry, unroll=unroll)

        def gather(q, _):
            image = []
            for c in range(3):
                halves = []
                for x in range(2):
                    s, d = back[4 * c + 2 * x, q], back[4 * c + 2 * x + 1, q]
                    halves.append((s - d) + upper(s + d))
                s, d = halves
                image.append((s - d) + right(s + d))
            finish(q, image)
            return 0

        lax.fori_loop(first, last, gather, 0)

    def misfit(q, image):
        glob_z = q + first_z
        inside = load_in & (glob_z >= 0) & (glob_z < total_z)
        return [jnp.where(inside, ext[3 + c, q], 0.0) - image[c] for c in range(3)]

    def update(q, image):
        r0, r1, r2 = misfit(q, image)
        i00, i11, i22, i01, i02, i12 = [inverse[k, q] for k in range(6)]
        cur[0, q] += i00 * r0 + i01 * r1 + i02 * r2
        cur[1, q] += i01 * r0 + i11 * r1 + i12 * r2
        cur[2, q] += i02 * r0 + i12 * r1 + i22 * r2

    def keep(q, image):
        for c, value in enumerate(misfit(q, image)):
            resid[c, q] = value

    for sweep in range(SWEEPS):
        apply(sweep + 1, planes - 1 - sweep, update)
    apply(LOW, LOW + size_z + 1, keep)

    for c in range(3):
        for z in range(size_z):
            smooth[c, z] = cur[c, LOW + z, LOW : LOW + size_y]

    parts_z, parts_y, parts_x = coarse.shape[1], size_y // 4, width // 4
    seg_after_z = ext[6, planes - 1, 0:1, :]
    seg_after_y = ext[6, planes - 1, 1:2, :]
    maps = []
    for k in range(parts_z):
        want = slab * parts_z + k
        weights = []
        places = []
        for z in range(size_z):
            weights.append(jnp.where(seg_z[z] == want, 1.0, 0.0).astype(F32))
            places.append(0.5 * (slab * size_z + z - 4 * want - 2).astype(F32))
        count = sum(weights)
        moment = sum(w * p for w, p in zip(weights, places))
        last = jnp.where((seg_after_z == want.astype(F32)) & (slab < lax.axis_size("slab") - 1), 1.0, 0.0)
        place = 0.5 * ((slab + 1) * size_z - 4 * want - 2).astype(F32)
        weights.append(last)
        places.append(place)
        count = count + last
        centre = (moment + last * place) / count
        scale = lax.rsqrt(count)
        sums = [jnp.zeros((rows, width), F32) for _ in range(3)]
        turns = [jnp.zeros((rows, width), F32) for _ in range(2)]
        for z in range(size_z + 1):
            for c in range(3):
                part = weights[z] * resid[c, LOW + z]
                sums[c] = sums[c] + part
                if c < 2:
                    turns[c] = turns[c] + places[z] * part
        maps += [scale * s for s in sums]
        maps += [scale * (turns[c] - centre * sums[c]) for c in range(2)]

    lane = lax.broadcasted_iota(jnp.int32, (2 * parts_y, rows), 1)
    part = lax.broadcasted_iota(jnp.int32, (2 * parts_y, rows), 0)
    turned = part >= parts_y
    part = jnp.where(turned, part - parts_y, part) + sub * parts_y
    segments = jnp.full((2 * parts_y, rows), -1, jnp.int32)
    for y in range(size_y):
        segments = jnp.where(lane == LOW + y, seg_y[y], segments)
    after = jnp.broadcast_to(seg_after_y[:, :rows], segments.shape)
    hit = (lane == LOW + size_y) & (after == part.astype(F32)) & (sub < lax.axis_size("sub") - 1)
    weight_y = jnp.where((segments == part) | hit, 1.0, 0.0)
    place_y = 0.5 * (lane + first_y - 4 * part - 2).astype(F32)
    count = jnp.sum(weight_y, axis=1, keepdims=True)
    centre = jnp.sum(weight_y * place_y, axis=1, keepdims=True) / count
    weight_y = weight_y * lax.rsqrt(count) * jnp.where(turned, place_y - centre, 1.0)

    square = (parts_y * parts_x, width)
    part = lax.rem(lax.broadcasted_iota(jnp.int32, square, 0), parts_x)
    weight_x = jnp.where(seg_x[...] == part, 1.0, 0.0)
    place_x = 0.5 * (lax.broadcasted_iota(jnp.int32, square, 1) - 4 * part - 2).astype(F32)
    count = jnp.sum(weight_x, axis=1, keepdims=True)
    centre = jnp.sum(weight_x * place_x, axis=1, keepdims=True) / count
    weight_x = weight_x * lax.rsqrt(count)
    weight_x = jnp.concatenate([weight_x, weight_x * (place_x - centre)], axis=0)

    wide = jnp.concatenate(maps, axis=1)
    by_y = jnp.dot(
        weight_y, wide, precision=lax.Precision.HIGHEST, preferred_element_type=F32
    )
    tall = jnp.concatenate(
        [by_y[:, width * k : width * (k + 1)] for k in range(len(maps))], axis=0
    )
    by_x = lax.dot_general(
        tall,
        weight_x,
        (((1,), (1,)), ((), ())),
        precision=lax.Precision.HIGHEST,
        preferred_element_type=F32,
    )
    spread = parts_y * parts_x
    pick = lax.broadcasted_iota(jnp.int32, (parts_y, spread), 0) == (
        lax.broadcasted_iota(jnp.int32, (parts_y, spread), 1) // parts_x
    )

    def chosen(k, turn_y, turn_x):
        start = (2 * k + turn_y) * parts_y
        block = by_x[start : start + parts_y, turn_x * spread : (turn_x + 1) * spread]
        return jnp.sum(jnp.where(pick, block, 0.0), axis=0, keepdims=True)

    for k in range(parts_z):
        b = 5 * k
        values = [chosen(b, 0, 0), chosen(b + 1, 0, 0), chosen(b + 2, 0, 0)]
        values.append(chosen(b + 2, 1, 0) - chosen(b + 4, 0, 0))
        values.append(chosen(b + 3, 0, 0) - chosen(b + 2, 0, 1))
        values.append(chosen(b + 1, 0, 1) - chosen(b, 1, 0))
        for c in range(6):
            coarse[c, k : k + 1, :] = values[c]


def on_device(field_init, load, modulus, seg_z, seg_y, seg_x):
    size_z, size_y, width = modulus.shape
    planes = size_z + LOW + HIGH
    rows = -(-(size_y + LOW + HIGH) // 8) * 8
    any_space = pl.BlockSpec(memory_space=pl.ANY)
    smem = pl.BlockSpec(memory_space=pltpu.SMEM)
    vmem = pl.BlockSpec(memory_space=pltpu.VMEM)
    ext = pl.pallas_call(
        halo_kernel,
        out_shape=jax.ShapeDtypeStruct((7, planes, rows, 1, width), F32),
        in_specs=[any_space, any_space, any_space, smem, smem],
        out_specs=any_space,
        scratch_shapes=[
            pltpu.VMEM((2, 1, width), F32),
            pltpu.SemaphoreType.DMA((len(SIDES), 4)),
            pltpu.SemaphoreType.DMA((len(SIDES), 4)),
            pltpu.SemaphoreType.DMA((3,)),
        ],
        compiler_params=pltpu.CompilerParams(collective_id=0, has_side_effects=True),
        name="halo",
    )(
        field_init.reshape(3, size_z, size_y, 1, width),
        load.reshape(3, size_z, size_y, 1, width),
        modulus.reshape(size_z, size_y, 1, width),
        seg_z,
        seg_y,
    )
    ext = ext.reshape(7, planes, rows, width)
    block = (planes, rows, width)
    smooth, coarse = pl.pallas_call(
        functools.partial(compute_kernel, unroll=1),
        out_shape=(
            jax.ShapeDtypeStruct((3, size_z, size_y, width), F32),
            jax.ShapeDtypeStruct((6, size_z // 4, size_y * width // 16), F32),
        ),
        in_specs=[smem, smem, vmem, vmem],
        out_specs=(vmem, vmem),
        scratch_shapes=[
            pltpu.VMEM((3, *block), F32),
            pltpu.VMEM(block, F32),
            pltpu.VMEM((6, *block), F32),
            pltpu.VMEM((12, *block), F32),
            pltpu.VMEM((12, *block), F32),
            pltpu.VMEM((3, *block), F32),
        ],
        compiler_params=pltpu.CompilerParams(vmem_limit_bytes=32 << 20),
        name="sweeps",
    )(seg_z, seg_y, seg_x.reshape(1, width), ext)
    return smooth, coarse


def solution(mesh):
    in_specs = (
        P(None, "slab", "sub", None),
        P(None, "slab", "sub", None),
        P("slab", "sub", None),
        P("slab"),
        P("sub"),
        P(),
    )
    out_specs = (P(None, "slab", "sub", None), P(None, "slab", "sub"))
    return jax.shard_map(
        on_device, mesh=mesh, in_specs=in_specs, out_specs=out_specs, check_vma=False
    )
```

profile of v0, /device:TPU:11, one launch (start us, length us, event | category | flops | bytes accessed | tf_op | source)
XLA Modules:
  0.0 29.9 jit_solution(374019235559291374)
XLA Ops:
  0.6 0.0 copy-start.2
  0.6 0.0 copy-start.1
  0.7 0.0 copy-start.3
  0.7 16.5 %halo.1 = f32[7,15,24,1,128]{4,3,2,1,0:T(1,128)} custom-call(f32[3,8,16,1,128]{4,3,2,1,0:T(1,128)} %bitcast.7, f32[3,8,16,1,128]{4,3,2,1,0:T(1,128)} %bitcast.8, f32[8,16,1,128]{3,2,1,0:T(1,128)} %bitcast.9, s32[8]{0:T(128)} %seg_z.3, s32[16]{0:T(128)} %seg_y.3), custom_call_target="tpu_custom_call" | custom-call | tf_op jit(solution)/shard_map/halo/pallas_call | solution.py:432
  17.2 0.0 copy-done.2
  17.2 0.0 copy-done.1
  17.2 0.0 copy-done.3
  17.2 0.0 copy-start
  17.2 1.3 %copy-done = f32[7,15,24,1,128]{4,3,2,1,0:T(1,128)S(1)} copy-done((f32[7,15,24,1,128]{4,3,2,1,0:T(1,128)S(1)}, f32[7,15,24,1,128]{4,3,2,1,0:T(1,128)}, u32[]{:S(2)}) %copy-start) | copy-done | bytes 1290264
  18.5 11.4 %sweeps.1 = (f32[3,8,16,128]{3,2,1,0:T(8,128)}, f32[6,2,128]{2,1,0:T(2,128)}) custom-call(s32[8]{0:T(128)S(1)} %copy-done.1, s32[16]{0:T(128)S(1)} %copy-done.2, s32[1,128]{1,0:T(1,128)S(1)} %bitcast.6, f32[7,15,24,128]{3,2,1,0:T(8,128)S(1)} %bitcast.5), custom_call_target="tpu_custom_call" | custom-call | tf_op jit(solution)/shard_map/sweeps/pallas_call | solution.py:454
Async XLA Ops:
  0.6 16.5 %copy-start.2 = (s32[16]{0:T(128)S(1)}, s32[16]{0:T(128)}, u32[]{:S(2)}) copy-start(s32[16]{0:T(128)} %seg_y.3) | copy-start | bytes 196
  0.6 16.5 %copy-start.1 = (s32[8]{0:T(128)S(1)}, s32[8]{0:T(128)}, u32[]{:S(2)}) copy-start(s32[8]{0:T(128)} %seg_z.3) | copy-start | bytes 100
  0.7 16.5 %copy-start.3 = (s32[128]{0:T(128)S(1)}, s32[128]{0:T(128)}, u32[]{:S(2)}) copy-start(s32[128]{0:T(128)} %param.11) | copy-start | bytes 1540
  17.2 1.3 %copy-start = (f32[7,15,24,1,128]{4,3,2,1,0:T(1,128)S(1)}, f32[7,15,24,1,128]{4,3,2,1,0:T(1,128)}, u32[]{:S(2)}) copy-start(f32[7,15,24,1,128]{4,3,2,1,0:T(1,128)} %halo.1) | copy-start | bytes 3870724
where the time goes:
time: 30.1 us; the launch traced here: 29.9 us
  Pallas kernels  27.9 us (93%)
  local copies, waits for them, and re-layouts  1.31 us (4%)
  between operations  0.7 us (2%)
    pallas_call x1, Pallas kernels, on_device(): pl.pallas_call(halo_kernel, out_shape=jax.ShapeDtypeStruct((7, planes, ro...  16.5 us
    pallas_call x1, Pallas kernels, on_device(): pl.pallas_call(functools.partial(compute_kernel, unroll=1), out_shape=(ja...  11.4 us
    unnamed x8, local copies, waits for them, and re-layouts  1.31 us

commit v1 on v0

v1 whole, which is shorter than its diff:
```python
import functools

import jax
import jax.numpy as jnp
from jax import lax
from jax.experimental import pallas as pl
from jax.experimental.pallas import tpu as pltpu
from jax.sharding import PartitionSpec as P

SWEEPS = 2
DAMPING = 0.6
PAD = 4
REACH = ((SWEEPS + 1, SWEEPS + 2), (SWEEPS, SWEEPS + 1), (SWEEPS + 1, SWEEPS + 1))
POISSON = 0.3
LAME = POISSON / ((1.0 + POISSON) * (1.0 - 2.0 * POISSON))
SHEAR = 0.5 / (1.0 + POISSON)
SIDES = ((-1, 0), (1, 0), (0, -1), (0, 1), (-1, -1), (-1, 1), (1, -1), (1, 1))
UNROLL = 2
MESH = pl.DeviceIdType.MESH
F32 = jnp.float32


def element_modes(lo, hi, e):
    def up(c, x, y):
        return lo[c][x][y] + hi[c][x][y]

    def diff(c, x, y):
        return hi[c][x][y] - lo[c][x][y]

    e_shear = e * (SHEAR / 16.0)
    e_shear2 = e * (SHEAR / 8.0)
    e_lame = e * (LAME / 16.0)
    e_lame3 = e * (LAME / 48.0)
    e_shear3 = e * (SHEAR / 48.0)
    e_last = e * ((LAME + 4.0 * SHEAR) / 144.0)
    out = [[[[None, None], [None, None]] for _ in range(2)] for _ in range(3)]

    n0, n1, n2 = up(0, 1, 0), up(1, 0, 1), diff(2, 0, 0)
    both = e_lame * (n0 + n1 + n2)
    out[0][1][0][0] = both + e_shear2 * n0
    out[1][0][1][0] = both + e_shear2 * n1
    out[2][0][0][1] = both + e_shear2 * n2

    both = e_shear * (up(0, 0, 1) + up(1, 1, 0))
    out[0][0][1][0] = both
    out[1][1][0][0] = both
    both = e_shear * (diff(0, 0, 0) + up(2, 1, 0))
    out[0][0][0][1] = both
    out[2][1][0][0] = both
    both = e_shear * (diff(1, 0, 0) + up(2, 0, 1))
    out[1][0][0][1] = both
    out[2][0][1][0] = both

    a, b = up(0, 1, 1), diff(2, 0, 1)
    both = e_lame3 * (a + b)
    out[0][1][1][0] = both + e_shear * a
    out[2][0][1][1] = both + e_shear * b
    a, b = diff(0, 1, 0), diff(1, 0, 1)
    both = e_lame3 * (a + b)
    out[0][1][0][1] = both + e_shear * a
    out[1][0][1][1] = both + e_shear * b
    a, b = up(1, 1, 1), diff(2, 1, 0)
    both = e_lame3 * (a + b)
    out[1][1][1][0] = both + e_shear * a
    out[2][1][0][1] = both + e_shear * b

    a, b, c = diff(0, 0, 1), diff(1, 1, 0), up(2, 1, 1)
    both = a + b + c
    out[0][0][1][1] = e_shear3 * (both + a)
    out[1][1][0][1] = e_shear3 * (both + b)
    out[2][1][1][0] = e_shear3 * (both + c)

    for c in range(3):
        out[c][1][1][1] = e_last * diff(c, 1, 1)
    return out


def kernel(
    seg_z,
    seg_y,
    seg_x,
    field,
    load,
    mod,
    smooth,
    coarse,
    packed,
    tails,
    halo,
    mark,
    marked,
    weights_x,
    cur,
    right_side,
    emod,
    inverse,
    modes,
    back,
    resid,
    send_sem,
    recv_sem,
    *,
    unroll,
):
    size_z, size_y, width = smooth.shape[1:]
    planes, rows = cur.shape[1], cur.shape[2]
    slab, sub = lax.axis_index("slab"), lax.axis_index("sub")
    slabs, subs = lax.axis_size("slab"), lax.axis_size("sub")
    total_z, total_y = size_z * slabs, size_y * subs
    parts_z, parts_y, parts_x = size_z // 4, size_y // 4, width // 4
    pairs = PAD // 2
    own_pairs = size_z // 2

    def present(dz, dy):
        there = jnp.bool_(True)
        if dz == 1:
            there = there & (slab < slabs - 1)
        if dz == -1:
            there = there & (slab > 0)
        if dy == 1:
            there = there & (sub < subs - 1)
        if dy == -1:
            there = there & (sub > 0)
        return there

    barrier = pltpu.get_barrier_semaphore()
    for dz, dy in SIDES:

        @pl.when(present(dz, dy))
        def _():
            pl.semaphore_signal(
                barrier, inc=1, device_id=(slab + dz, sub + dy), device_id_type=MESH
            )

    first_half = lax.broadcasted_iota(jnp.int32, (8, width), 0) < PAD

    def unit(refs, k):
        return refs[k // 3].at[k % 3] if k < 6 else refs[2]

    inputs = (field, load, mod)

    def pack(i, _):
        for k in range(7):
            src = unit(inputs, k)
            a, b = src[2 * i, 0:8], src[2 * i + 1, 0:8]
            packed[0, k, i] = jnp.where(first_half, a, pltpu.roll(b, PAD, 0))
            a, b = src[2 * i, size_y - 8 : size_y], src[2 * i + 1, size_y - 8 : size_y]
            packed[1, k, i] = jnp.where(first_half, pltpu.roll(b, PAD, 0), a)
        return 0

    lax.fori_loop(0, own_pairs, pack, 0)
    mark[0] = jnp.full((8, width), seg_z[0].astype(F32))
    mark[1] = jnp.full((8, width), seg_y[0].astype(F32))

    peers_z = 3 - (slab == 0).astype(jnp.int32) - (slab == slabs - 1).astype(jnp.int32)
    peers_y = 3 - (sub == 0).astype(jnp.int32) - (sub == subs - 1).astype(jnp.int32)
    pl.semaphore_wait(barrier, peers_z * peers_y - 1)

    copies = {}
    for side, (dz, dy) in enumerate(SIDES):
        group = []
        if dy == 0:
            for k, src in enumerate(inputs):
                low, high = REACH[k]
                if dz == 1:
                    start, to, count = size_z - low, PAD - low, low
                else:
                    start, to, count = 0, PAD + size_z, high
                if k < 2:
                    group.append(
                        (
                            src.at[:, pl.ds(start, count)],
                            halo.at[pl.ds(3 * k, 3), pl.ds(to, count)],
                        )
                    )
                else:
                    group.append((src.at[pl.ds(start, count)], halo.at[6, pl.ds(to, count)]))
        else:
            which = 0 if dy == -1 else 1
            start, to, count = {
                -1: (0, pairs + own_pairs, pairs),
                0: (0, pairs, own_pairs),
                1: (own_pairs - pairs, 0, pairs),
            }[dz]
            group.append(
                (
                    packed.at[which, :, pl.ds(start, count)],
                    tails.at[which, :, pl.ds(to, count)],
                )
            )
        if (dz, dy) == (-1, 0):
            group.append((mark.at[0], marked.at[0]))
        if (dz, dy) == (0, -1):
            group.append((mark.at[1], marked.at[1]))
        group = [
            pltpu.make_async_remote_copy(
                src_ref=from_ref,
                dst_ref=to_ref,
                send_sem=send_sem.at[side, k],
                recv_sem=recv_sem.at[side, k],
                device_id=(slab + dz, sub + dy),
                device_id_type=MESH,
            )
            for k, (from_ref, to_ref) in enumerate(group)
        ]
        copies[dz, dy] = group

        @pl.when(present(dz, dy))
        def _():
            for copy in group:
                copy.start()

    def arrived(sides):
        for dz, dy in sides:

            @pl.when(present(-dz, -dy))
            def _():
                for copy in copies[dz, dy]:
                    copy.wait_recv()

    square = (parts_y * parts_x, width)
    part = lax.rem(lax.broadcasted_iota(jnp.int32, square, 0), parts_x)
    weight_x = jnp.where(seg_x[...] == part, 1.0, 0.0)
    place_x = 0.5 * (lax.broadcasted_iota(jnp.int32, square, 1) - 4 * part - 2).astype(F32)
    count = jnp.sum(weight_x, axis=1, keepdims=True)
    centre = jnp.sum(weight_x * place_x, axis=1, keepdims=True) / count
    weight_x = weight_x * lax.rsqrt(count)
    weights_x[0 : square[0]] = weight_x
    weights_x[square[0] : 2 * square[0]] = weight_x * (place_x - centre)

    first_z = slab * size_z - PAD
    row = lax.broadcasted_iota(jnp.int32, (rows, width), 0)
    column = lax.broadcasted_iota(jnp.int32, (rows, width), 1)
    near = jnp.where(row < size_y + PAD, row, row - rows)
    glob_y = near + sub * size_y
    rows_in = (glob_y >= 0) & (glob_y < total_y)
    elements_in = (
        rows_in
        & (glob_y < total_y - 1)
        & (near >= -SWEEPS - 1)
        & (near < size_y + SWEEPS + 1)
        & (column < width - 1)
    )

    def left(v):
        return pltpu.roll(v, v.shape[1] - 1, 1)

    def right(v):
        return pltpu.roll(v, 1, 1)

    def lower(v):
        return pltpu.roll(v, v.shape[0] - 1, 0)

    def upper(v):
        return pltpu.roll(v, 1, 0)

    def stage(i, refs, shift):
        for k in range(7):
            src = unit(refs, k) if shift else halo.at[k]
            above, below = tails[0, k, i], tails[1, k, i]
            ends = (
                jnp.where(first_half, above, below),
                pltpu.roll(jnp.where(first_half, below, above), PAD, 0),
            )
            for odd in range(2):
                q = 2 * i + odd
                glob_z = q + first_z
                value = jnp.concatenate([src[q - shift], ends[odd]], axis=0)
                if k < 6:
                    keep = rows_in & (glob_z >= 0) & (glob_z < total_z)
                    value = jnp.where(keep, value, 0.0)
                    if k < 3:
                        cur[k, q] = value
                    else:
                        right_side[k - 3, q] = value
                else:
                    keep = elements_in & (glob_z >= 0) & (glob_z < total_z - 1)
                    emod[q] = jnp.where(keep, value, 0.0)

    def stage_own(i, _):
        stage(i, inputs, PAD)
        return 0

    def stage_halo(i, _):
        stage(i, None, 0)
        return 0

    def sum_modes(q):
        e = emod[q]
        r = right(e)
        s, d = e + r, r - e
        us, ud = upper(s), upper(d)
        return s + us, us - s, d + ud, ud - d

    def invert(q, before):
        now = sum_modes(q)
        main = (LAME + 4.0 * SHEAR) / 9.0
        side = (LAME + SHEAR) / 12.0
        p = main * (now[0] + before[0])
        xy = side * (now[3] + before[3])
        xz = side * (before[2] - now[2])
        yz = side * (before[1] - now[1])
        pp = p * p
        c00 = pp - yz * yz
        c11 = pp - xz * xz
        c22 = pp - xy * xy
        c01 = xz * yz - xy * p
        c02 = xy * yz - xz * p
        c12 = xy * xz - yz * p
        det = p * c00 + xy * c01 + xz * c02
        scale = DAMPING / jnp.where(p > 0.0, det, 1.0)
        for k, entry in enumerate((c00, c11, c22, c01, c02, c12)):
            inverse[k, q] = entry * scale
        return now

    def forward(q, _):
        for c in range(3):
            u = cur[c, q]
            a = left(u)
            for x, t in enumerate((u + a, a - u)):
                b = lower(t)
                modes[4 * c + 2 * x, q] = t + b
                modes[4 * c + 2 * x + 1, q] = b - t
        return 0

    tiles = [pl.ds(8 * tile, 8) for tile in range(rows // 8)]

    def elements(first, last, begin):
        for at in tiles:

            def element(q, carry):
                lo = [
                    [[modes[4 * c + 2 * x + y, q, at] for y in range(2)] for x in range(2)]
                    for c in range(3)
                ]
                hi = [
                    [[modes[4 * c + 2 * x + y, q + 1, at] for y in range(2)] for x in range(2)]
                    for c in range(3)
                ]
                out = element_modes(lo, hi, emod[q, at])
                after = []
                for c in range(3):
                    for x in range(2):
                        for y in range(2):
                            k = 4 * c + 2 * x + y
                            total, change = out[c][x][y]
                            if total is None:
                                back[k, q, at] = carry[k] - change
                                after.append(change)
                            else:
                                back[k, q, at] = carry[k] + (total - change)
                                after.append(total + change)
                return tuple(after)

            if begin:
                carry = tuple(back[k, first, at] for k in range(12))
            else:
                carry = (jnp.zeros((8, width), F32),) * 12
            carry = lax.fori_loop(first, last, element, carry, unroll=unroll)
            for k in range(12):
                back[k, last, at] = carry[k]

    def image(q):
        result = []
        for c in range(3):
            halves = []
            for x in range(2):
                s, d = back[4 * c + 2 * x, q], back[4 * c + 2 * x + 1, q]
                halves.append((s - d) + upper(s + d))
            s, d = halves
            result.append((s - d) + right(s + d))
        return result

    def misfit(q):
        moved = image(q)
        return [right_side[c, q] - moved[c] for c in range(3)]

    def update(q, _):
        r0, r1, r2 = misfit(q)
        i00, i11, i22, i01, i02, i12 = [inverse[k, q] for k in range(6)]
        cur[0, q] += i00 * r0 + i01 * r1 + i02 * r2
        cur[1, q] += i01 * r0 + i11 * r1 + i12 * r2
        cur[2, q] += i02 * r0 + i12 * r1 + i22 * r2
        return forward(q, 0)

    def keep(q, _):
        for c, value in enumerate(misfit(q)):
            resid[c, q] = value
        return 0

    top = PAD + size_z
    arrived([(0, -1), (0, 1)])
    lax.fori_loop(pairs, pairs + own_pairs, stage_own, 0)
    lax.fori_loop(PAD, top, forward, 0)
    elements(PAD, top - 1, False)
    lax.fori_loop(PAD + 1, top - 1, invert, sum_modes(PAD))
    arrived([side for side in SIDES if side[0] != 0])
    lax.fori_loop(0, pairs, stage_halo, 0)
    lax.fori_loop(pairs + own_pairs, 2 * pairs + own_pairs, stage_halo, 0)
    lax.fori_loop(1, PAD, forward, 0)
    lax.fori_loop(top, planes, forward, 0)
    held = [[back[k, PAD, at] for at in tiles] for k in range(12)]
    elements(1, PAD, False)
    for k in range(12):
        for at, value in zip(tiles, held[k]):
            back[k, PAD, at] += value
    elements(top - 1, planes - 1, True)
    lax.fori_loop(2, PAD + 1, invert, sum_modes(1))
    lax.fori_loop(top - 1, planes - 1, invert, sum_modes(top - 2))
    lax.fori_loop(2, planes - 1, update, 0)
    for sweep in range(1, SWEEPS):
        elements(sweep + 1, planes - 1 - sweep, False)
        lax.fori_loop(sweep + 2, planes - 1 - sweep, update, 0)
    elements(PAD - 1, top + 1, False)
    lax.fori_loop(PAD, top + 1, keep, 0)
    for c in range(3):
        for z in range(size_z):
            smooth[c, z] = cur[c, PAD + z, 0:size_y]

    seg_after_z = marked[0, 0:1, :]
    seg_after_y = marked[1, 0:1, :]
    maps = []
    for k in range(parts_z):
        want = slab * parts_z + k
        weights = []
        places = []
        for z in range(size_z):
            weights.append(jnp.where(seg_z[z] == want, 1.0, 0.0).astype(F32))
            places.append(0.5 * (slab * size_z + z - 4 * want - 2).astype(F32))
        count = sum(weights)
        moment = sum(w * p for w, p in zip(weights, places))
        last = jnp.where((seg_after_z == want.astype(F32)) & (slab < slabs - 1), 1.0, 0.0)
        place = 0.5 * ((slab + 1) * size_z - 4 * want - 2).astype(F32)
        weights.append(last)
        places.append(place)
        count = count + last
        centre = (moment + last * place) / count
        scale = lax.rsqrt(count)
        sums = [jnp.zeros((rows, width), F32) for _ in range(3)]
        turns = [jnp.zeros((rows, width), F32) for _ in range(2)]
        for z in range(size_z + 1):
            for c in range(3):
                part = weights[z] * resid[c, PAD + z]
                sums[c] = sums[c] + part
                if c < 2:
                    turns[c] = turns[c] + places[z] * part
        maps += [scale * s for s in sums]
        maps += [scale * (turns[c] - centre * sums[c]) for c in range(2)]

    lane = lax.broadcasted_iota(jnp.int32, (2 * parts_y, rows), 1)
    part = lax.broadcasted_iota(jnp.int32, (2 * parts_y, rows), 0)
    turned = part >= parts_y
    part = jnp.where(turned, part - parts_y, part) + sub * parts_y
    segments = jnp.full((2 * parts_y, rows), -1, jnp.int32)
    for y in range(size_y):
        segments = jnp.where(lane == y, seg_y[y], segments)
    after = jnp.broadcast_to(seg_after_y[:, :rows], segments.shape)
    hit = (lane == size_y) & (after == part.astype(F32)) & (sub < subs - 1)
    weight_y = jnp.where((segments == part) | hit, 1.0, 0.0)
    place_y = 0.5 * (lane + sub * size_y - 4 * part - 2).astype(F32)
    count = jnp.sum(weight_y, axis=1, keepdims=True)
    centre = jnp.sum(weight_y * place_y, axis=1, keepdims=True) / count
    weight_y = weight_y * lax.rsqrt(count) * jnp.where(turned, place_y - centre, 1.0)

    wide = jnp.concatenate(maps, axis=1)
    by_y = jnp.dot(
        weight_y, wide, precision=lax.Precision.HIGHEST, preferred_element_type=F32
    )
    tall = jnp.concatenate(
        [by_y[:, width * k : width * (k + 1)] for k in range(len(maps))], axis=0
    )
    by_x = lax.dot_general(
        tall,
        weights_x[...],
        (((1,), (1,)), ((), ())),
        precision=lax.Precision.HIGHEST,
        preferred_element_type=F32,
    )
    spread = parts_y * parts_x
    pick = lax.broadcasted_iota(jnp.int32, (parts_y, spread), 0) == (
        lax.broadcasted_iota(jnp.int32, (parts_y, spread), 1) // parts_x
    )

    def chosen(k, turn_y, turn_x):
        start = (2 * k + turn_y) * parts_y
        block = by_x[start : start + parts_y, turn_x * spread : (turn_x + 1) * spread]
        return jnp.sum(jnp.where(pick, block, 0.0), axis=0, keepdims=True)

    for k in range(parts_z):
        b = 5 * k
        values = [chosen(b, 0, 0), chosen(b + 1, 0, 0), chosen(b + 2, 0, 0)]
        values.append(chosen(b + 2, 1, 0) - chosen(b + 4, 0, 0))
        values.append(chosen(b + 3, 0, 0) - chosen(b + 2, 0, 1))
        values.append(chosen(b + 1, 0, 1) - chosen(b, 1, 0))
        for c in range(6):
            coarse[c, k : k + 1, :] = values[c]

    for dz, dy in SIDES:

        @pl.when(present(dz, dy))
        def _():
            for copy in copies[dz, dy]:
                copy.wait_send()


def on_device(field_init, load, modulus, seg_z, seg_y, seg_x):
    size_z, size_y, width = modulus.shape
    planes = size_z + 2 * PAD
    rows = size_y + 2 * PAD
    smem = pl.BlockSpec(memory_space=pltpu.SMEM)
    vmem = pl.BlockSpec(memory_space=pltpu.VMEM)
    block = (planes, rows, width)
    smooth, coarse = pl.pallas_call(
        functools.partial(kernel, unroll=UNROLL),
        out_shape=(
            jax.ShapeDtypeStruct((3, size_z, size_y, width), F32),
            jax.ShapeDtypeStruct((6, size_z // 4, size_y * width // 16), F32),
        ),
        in_specs=[smem, smem, vmem, vmem, vmem, vmem],
        out_specs=(vmem, vmem),
        scratch_shapes=[
            pltpu.VMEM((2, 7, size_z // 2, 8, width), F32),
            pltpu.VMEM((2, 7, planes // 2, 8, width), F32),
            pltpu.VMEM((7, planes, size_y, width), F32),
            pltpu.VMEM((2, 8, width), F32),
            pltpu.VMEM((2, 8, width), F32),
            pltpu.VMEM((size_y * width // 8, width), F32),
            pltpu.VMEM((3, *block), F32),
            pltpu.VMEM((3, *block), F32),
            pltpu.VMEM(block, F32),
            pltpu.VMEM((6, *block), F32),
            pltpu.VMEM((12, *block), F32),
            pltpu.VMEM((12, *block), F32),
            pltpu.VMEM((3, *block), F32),
            pltpu.SemaphoreType.DMA((len(SIDES), 4)),
            pltpu.SemaphoreType.DMA((len(SIDES), 4)),
        ],
        compiler_params=pltpu.CompilerParams(
            collective_id=0, has_side_effects=True, vmem_limit_bytes=32 << 20
        ),
        name="sweeps",
    )(seg_z, seg_y, seg_x.reshape(1, width), field_init, load, modulus)
    return smooth, coarse


def solution(mesh):
    in_specs = (
        P(None, "slab", "sub", None),
        P(None, "slab", "sub", None),
        P("slab", "sub", None),
        P("slab"),
        P("sub"),
        P(),
    )
    out_specs = (P(None, "slab", "sub", None), P(None, "slab", "sub"))
    return jax.shard_map(
        on_device, mesh=mesh, in_specs=in_specs, out_specs=out_specs, check_vma=False
    )
```

time: 30.1 us -> 26.3 us (0.87)
  Pallas kernels: 27.9 us -> 20.8 us
  local copies, waits for them, and re-layouts: 1.31 us -> 4.63 us
    pallas_call x2 -> x1, Pallas kernels: 27.9 us -> 20.8 us  [on_device(): pl.pallas_call(functools.partial(kernel, unroll=UNROLL), out_shape=(jax.S...]
    unnamed x8 -> x14, local copies, waits for them, and re-layouts: 1.31 us -> 4.63 us
where the time goes in v1:
time: 26.3 us; the launch traced here: 26.1 us
  Pallas kernels  20.8 us (79%)
  local copies, waits for them, and re-layouts  4.63 us (18%)
  between operations  0.67 us (3%)
    pallas_call x1, Pallas kernels, on_device(): pl.pallas_call(functools.partial(kernel, unroll=UNROLL), out_shape=(jax.S...  20.8 us
    unnamed x14, local copies, waits for them, and re-layouts  4.63 us

profile of v1, /device:TPU:11, one launch (start us, length us, event | category | flops | bytes accessed | tf_op | source)
XLA Modules:
  0.0 26.1 jit_solution(13596085922323489402)
XLA Ops:
  0.6 0.0 copy-start.5
  0.6 0.0 copy-start.4
  0.7 0.0 copy-start.3
  0.7 0.6 %copy-done.5 = s32[128]{0:T(128)S(1)} copy-done((s32[128]{0:T(128)S(1)}, s32[128]{0:T(128)}, u32[]{:S(2)}) %copy-start.5) | copy-done | bytes 536
  1.3 0.0 copy-done.4
  1.3 0.0 copy-done.3
  1.3 0.0 copy-start
  1.3 0.9 %copy-done = f32[3,8,16,128]{3,2,1,0:T(8,128)S(1)} copy-done((f32[3,8,16,128]{3,2,1,0:T(8,128)S(1)}, f32[3,8,16,128]{3,2,1,0:T(8,128)}, u32[]{:S(2)}) %copy-start) | copy-done | bytes 196632
  2.2 0.0 copy-start.1
  2.2 0.9 %copy-done.1 = f32[3,8,16,128]{3,2,1,0:T(8,128)S(1)} copy-done((f32[3,8,16,128]{3,2,1,0:T(8,128)S(1)}, f32[3,8,16,128]{3,2,1,0:T(8,128)}, u32[]{:S(2)}) %copy-start.1) | copy-done | bytes 196632
  3.2 0.0 copy-start.2
  3.2 0.8 %copy-done.2 = f32[8,16,128]{2,1,0:T(8,128)S(1)} copy-done((f32[8,16,128]{2,1,0:T(8,128)S(1)}, f32[8,16,128]{2,1,0:T(8,128)}, u32[]{:S(2)}) %copy-start.2) | copy-done | bytes 65560
  4.0 20.8 %sweeps.1 = (f32[3,8,16,128]{3,2,1,0:T(8,128)S(1)}, f32[6,2,128]{2,1,0:T(2,128)S(1)}) custom-call(s32[8]{0:T(128)S(1)} %copy-done.3, s32[16]{0:T(128)S(1)} %copy-done.4, s32[1,128]{1,0:T(1,128)S(1)} %bitcast.1, f32[3,8,16,128]{3,2,1,0:T(8,128)S(1)} %copy-done, f32[3,8,16,128]{3,2,1,0:T(8,128)S(1)} %copy-done.1, f32[8,16,128]{2,1,0:T(8,128)S(1)} %copy-done.2), custom_call_target="tpu_custom_call" | custom-call | tf_op jit(solution)/shard_map/sweeps/pallas_call | solution.py:513
  24.8 0.7 %copy.10 = f32[3,8,16,128]{3,2,1,0:T(8,128)} copy(f32[3,8,16,128]{3,2,1,0:T(8,128)S(1)} %get-tuple-element.4) | data formatting | bytes 393216
  25.5 0.6 %copy.11 = f32[6,2,128]{2,1,0:T(2,128)} copy(f32[6,2,128]{2,1,0:T(2,128)S(1)} %get-tuple-element.5) | data formatting | bytes 12288
Async XLA Ops:
  0.6 0.7 %copy-start.5 = (s32[128]{0:T(128)S(1)}, s32[128]{0:T(128)}, u32[]{:S(2)}) copy-start(s32[128]{0:T(128)} %param.11) | copy-start | bytes 1540
  0.6 0.7 %copy-start.4 = (s32[16]{0:T(128)S(1)}, s32[16]{0:T(128)}, u32[]{:S(2)}) copy-start(s32[16]{0:T(128)} %seg_y.1) | copy-start | bytes 196
  0.7 0.7 %copy-start.3 = (s32[8]{0:T(128)S(1)}, s32[8]{0:T(128)}, u32[]{:S(2)}) copy-start(s32[8]{0:T(128)} %seg_z.1) | copy-start | bytes 100
  1.3 0.9 %copy-start = (f32[3,8,16,128]{3,2,1,0:T(8,128)S(1)}, f32[3,8,16,128]{3,2,1,0:T(8,128)}, u32[]{:S(2)}) copy-start(f32[3,8,16,128]{3,2,1,0:T(8,128)} %field.1) | copy-start | bytes 589828
  2.2 0.9 %copy-start.1 = (f32[3,8,16,128]{3,2,1,0:T(8,128)S(1)}, f32[3,8,16,128]{3,2,1,0:T(8,128)}, u32[]{:S(2)}) copy-start(f32[3,8,16,128]{3,2,1,0:T(8,128)} %load.1) | copy-start | bytes 589828
  3.2 0.8 %copy-start.2 = (f32[8,16,128]{2,1,0:T(8,128)S(1)}, f32[8,16,128]{2,1,0:T(8,128)}, u32[]{:S(2)}) copy-start(f32[8,16,128]{2,1,0:T(8,128)} %mod.1) | copy-start | bytes 196612

commit v2 on v1

--- a/solution.py
+++ b/solution.py
@@ -75,15 +75,28 @@
     return out
 
 
+def flat(first, last, body, carry=0):
+    for q in range(first, last):
+        carry = body(q, carry)
+    return carry
+
+
 def kernel(
+    seg_z_hbm,
+    seg_y_hbm,
+    seg_x_hbm,
+    field_hbm,
+    load_hbm,
+    mod_hbm,
+    smooth,
+    coarse,
     seg_z,
     seg_y,
     seg_x,
     field,
     load,
     mod,
-    smooth,
-    coarse,
+    own_sem,
     packed,
     tails,
     halo,
@@ -132,6 +145,24 @@
                 barrier, inc=1, device_id=(slab + dz, sub + dy), device_id_type=MESH
             )
 
+    own = [
+        pltpu.make_async_copy(src, dst, own_sem.at[k])
+        for k, (src, dst) in enumerate(
+            (
+                (field_hbm, field),
+                (load_hbm, load),
+                (mod_hbm, mod),
+                (seg_z_hbm, seg_z),
+                (seg_y_hbm, seg_y),
+                (seg_x_hbm, seg_x),
+            )
+        )
+    ]
+    for copy in own:
+        copy.start()
+    for copy in own:
+        copy.wait()
+
     first_half = lax.broadcasted_iota(jnp.int32, (8, width), 0) < PAD
 
     def unit(refs, k):
@@ -148,7 +179,7 @@
             packed[1, k, i] = jnp.where(first_half, pltpu.roll(b, PAD, 0), a)
         return 0
 
-    lax.fori_loop(0, own_pairs, pack, 0)
+    flat(0, own_pairs, pack)
     mark[0] = jnp.full((8, width), seg_z[0].astype(F32))
     mark[1] = jnp.full((8, width), seg_y[0].astype(F32))
 
@@ -390,29 +421,29 @@
 
     top = PAD + size_z
     arrived([(0, -1), (0, 1)])
-    lax.fori_loop(pairs, pairs + own_pairs, stage_own, 0)
-    lax.fori_loop(PAD, top, forward, 0)
+    flat(pairs, pairs + own_pairs, stage_own)
+    flat(PAD, top, forward)
     elements(PAD, top - 1, False)
-    lax.fori_loop(PAD + 1, top - 1, invert, sum_modes(PAD))
+    flat(PAD + 1, top - 1, invert, sum_modes(PAD))
     arrived([side for side in SIDES if side[0] != 0])
-    lax.fori_loop(0, pairs, stage_halo, 0)
-    lax.fori_loop(pairs + own_pairs, 2 * pairs + own_pairs, stage_halo, 0)
-    lax.fori_loop(1, PAD, forward, 0)
-    lax.fori_loop(top, planes, forward, 0)
+    flat(0, pairs, stage_halo)
+    flat(pairs + own_pairs, 2 * pairs + own_pairs, stage_halo)
+    flat(1, PAD, forward)
+    flat(top, planes, forward)
     held = [[back[k, PAD, at] for at in tiles] for k in range(12)]
     elements(1, PAD, False)
     for k in range(12):
         for at, value in zip(tiles, held[k]):
             back[k, PAD, at] += value
     elements(top - 1, planes - 1, True)
-    lax.fori_loop(2, PAD + 1, invert, sum_modes(1))
-    lax.fori_loop(top - 1, planes - 1, invert, sum_modes(top - 2))
-    lax.fori_loop(2, planes - 1, update, 0)
+    flat(2, PAD + 1, invert, sum_modes(1))
+    flat(top - 1, planes - 1, invert, sum_modes(top - 2))
+    flat(2, planes - 1, update)
     for sweep in range(1, SWEEPS):
         elements(sweep + 1, planes - 1 - sweep, False)
-        lax.fori_loop(sweep + 2, planes - 1 - sweep, update, 0)
+        flat(sweep + 2, planes - 1 - sweep, update)
     elements(PAD - 1, top + 1, False)
-    lax.fori_loop(PAD, top + 1, keep, 0)
+    flat(PAD, top + 1, keep)
     for c in range(3):
         for z in range(size_z):
             smooth[c, z] = cur[c, PAD + z, 0:size_y]
@@ -507,7 +538,7 @@
     size_z, size_y, width = modulus.shape
     planes = size_z + 2 * PAD
     rows = size_y + 2 * PAD
-    smem = pl.BlockSpec(memory_space=pltpu.SMEM)
+    hbm = pl.BlockSpec(memory_space=pltpu.HBM)
     vmem = pl.BlockSpec(memory_space=pltpu.VMEM)
     block = (planes, rows, width)
     smooth, coarse = pl.pallas_call(
@@ -516,9 +547,16 @@
             jax.ShapeDtypeStruct((3, size_z, size_y, width), F32),
             jax.ShapeDtypeStruct((6, size_z // 4, size_y * width // 16), F32),
         ),
-        in_specs=[smem, smem, vmem, vmem, vmem, vmem],
+        in_specs=[hbm] * 6,
         out_specs=(vmem, vmem),
         scratch_shapes=[
+            pltpu.SMEM(seg_z.shape, jnp.int32),
+            pltpu.SMEM(seg_y.shape, jnp.int32),
+            pltpu.VMEM((1, width), jnp.int32),
+            pltpu.VMEM(field_init.shape, F32),
+            pltpu.VMEM(load.shape, F32),
+            pltpu.VMEM(modulus.shape, F32),
+            pltpu.SemaphoreType.DMA((6,)),
             pltpu.VMEM((2, 7, size_z // 2, 8, width), F32),
             pltpu.VMEM((2, 7, planes // 2, 8, width), F32),
             pltpu.VMEM((7, planes, size_y, width), F32),
@@ -536,7 +574,7 @@
             pltpu.SemaphoreType.DMA((len(SIDES), 4)),
         ],
         compiler_params=pltpu.CompilerParams(
-            collective_id=0, has_side_effects=True, vmem_limit_bytes=32 << 20
+            collective_id=0, has_side_effects=True, vmem_limit_bytes=(64 << 20) - (64 << 10)
         ),
         name="sweeps",
     )(seg_z, seg_y, seg_x.reshape(1, width), field_init, load, modulus)

time: 26.3 us -> 19.5 us (0.74)
  Pallas kernels: 20.8 us -> 16.5 us
  local copies, waits for them, and re-layouts: 4.63 us -> 2.22 us
    pallas_call x1, Pallas kernels: 20.8 us -> 16.5 us  [on_device(): pl.pallas_call(functools.partial(kernel, unroll=UNROLL), out_shape=(jax.S...]
    unnamed x14 -> x4, local copies, waits for them, and re-layouts: 4.63 us -> 2.22 us
where the time goes in v2:
time: 19.5 us; the launch traced here: 19.4 us
  Pallas kernels  16.5 us (85%)
  local copies, waits for them, and re-layouts  2.22 us (11%)
  between operations  0.65 us (3%)
    pallas_call x1, Pallas kernels, on_device(): pl.pallas_call(functools.partial(kernel, unroll=UNROLL), out_shape=(jax.S...  16.5 us
    unnamed x4, local copies, waits for them, and re-layouts  2.22 us

profile of v2, /device:TPU:11, one launch (start us, length us, event | category | flops | bytes accessed | tf_op | source)
XLA Modules:
  0.0 19.4 jit_solution(10263529597623876040)
XLA Ops:
  0.6 16.5 %sweeps.1 = (f32[3,8,16,128]{3,2,1,0:T(8,128)}, f32[6,2,128]{2,1,0:T(2,128)}) custom-call(s32[8]{0:T(128)} %seg_z_hbm.1, s32[16]{0:T(128)} %seg_y_hbm.1, s32[1,128]{1,0:T(1,128)} %bitcast.1, f32[3,8,16,128]{3,2,1,0:T(8,128)} %field_hbm.1, f32[3,8,16,128]{3,2,1,0:T(8,128)} %load_hbm.1, f32[8,16,128]{2,1,0:T(8,128)} %mod_hbm.1), custom_call_target="tpu_custom_call" | custom-call | tf_op jit(solution)/shard_map/sweeps/pallas_call | solution.py:544
  17.1 0.0 copy-start
  17.2 1.6 %copy.10 = f32[3,8,16,128]{3,2,1,0:T(8,128)} copy(f32[3,8,16,128]{3,2,1,0:T(8,128)} %get-tuple-element.4) | data formatting | bytes 393216
  18.8 0.0 copy-done
  18.8 0.6 %copy.11 = f32[6,2,128]{2,1,0:T(2,128)} copy(f32[6,2,128]{2,1,0:T(2,128)S(1)} %copy-done) | data formatting | bytes 12288
Async XLA Ops:
  17.1 1.6 %copy-start = (f32[6,2,128]{2,1,0:T(2,128)S(1)}, f32[6,2,128]{2,1,0:T(2,128)}, u32[]{:S(2)}) copy-start(f32[6,2,128]{2,1,0:T(2,128)} %get-tuple-element.5) | copy-start | bytes 18436

commit v3 on v2

--- a/solution.py
+++ b/solution.py
@@ -344,28 +344,31 @@
             inverse[k, q] = entry * scale
         return now
 
-    def forward(q, _):
+    def forward(q, sweep):
         for c in range(3):
             u = cur[c, q]
             a = left(u)
             for x, t in enumerate((u + a, a - u)):
                 b = lower(t)
-                modes[4 * c + 2 * x, q] = t + b
-                modes[4 * c + 2 * x + 1, q] = b - t
-        return 0
+                modes[sweep, 4 * c + 2 * x, q] = t + b
+                modes[sweep, 4 * c + 2 * x + 1, q] = b - t
+        return sweep
 
     tiles = [pl.ds(8 * tile, 8) for tile in range(rows // 8)]
 
-    def elements(first, last, begin):
+    def elements(sweep, first, last, begin, add):
         for at in tiles:
 
             def element(q, carry):
                 lo = [
-                    [[modes[4 * c + 2 * x + y, q, at] for y in range(2)] for x in range(2)]
+                    [[modes[sweep, 4 * c + 2 * x + y, q, at] for y in range(2)] for x in range(2)]
                     for c in range(3)
                 ]
                 hi = [
-                    [[modes[4 * c + 2 * x + y, q + 1, at] for y in range(2)] for x in range(2)]
+                    [
+                        [modes[sweep, 4 * c + 2 * x + y, q + 1, at] for y in range(2)]
+                        for x in range(2)
+                    ]
                     for c in range(3)
                 ]
                 out = element_modes(lo, hi, emod[q, at])
@@ -376,74 +379,72 @@
                             k = 4 * c + 2 * x + y
                             total, change = out[c][x][y]
                             if total is None:
-                                back[k, q, at] = carry[k] - change
+                                back[sweep, k, q, at] = carry[k] - change
                                 after.append(change)
                             else:
-                                back[k, q, at] = carry[k] + (total - change)
+                                back[sweep, k, q, at] = carry[k] + (total - change)
                                 after.append(total + change)
                 return tuple(after)
 
             if begin:
-                carry = tuple(back[k, first, at] for k in range(12))
+                carry = tuple(back[sweep, k, first, at] for k in range(12))
             else:
                 carry = (jnp.zeros((8, width), F32),) * 12
             carry = lax.fori_loop(first, last, element, carry, unroll=unroll)
             for k in range(12):
-                back[k, last, at] = carry[k]
-
-    def image(q):
+                if add:
+                    back[sweep, k, last, at] += carry[k]
+                else:
+                    back[sweep, k, last, at] = carry[k]
+
+    def image(sweep, q):
         result = []
         for c in range(3):
             halves = []
             for x in range(2):
-                s, d = back[4 * c + 2 * x, q], back[4 * c + 2 * x + 1, q]
+                k = 4 * c + 2 * x
+                s, d = back[sweep, k, q], back[sweep, k + 1, q]
                 halves.append((s - d) + upper(s + d))
             s, d = halves
             result.append((s - d) + right(s + d))
         return result
 
-    def misfit(q):
-        moved = image(q)
-        return [right_side[c, q] - moved[c] for c in range(3)]
-
-    def update(q, _):
-        r0, r1, r2 = misfit(q)
+    def finish(q, sweep):
+        moved = image(sweep, q)
+        r0, r1, r2 = [right_side[c, q] - moved[c] for c in range(3)]
+        if sweep == SWEEPS:
+            for c, value in enumerate((r0, r1, r2)):
+                resid[c, q] = value
+            return sweep
         i00, i11, i22, i01, i02, i12 = [inverse[k, q] for k in range(6)]
         cur[0, q] += i00 * r0 + i01 * r1 + i02 * r2
         cur[1, q] += i01 * r0 + i11 * r1 + i12 * r2
         cur[2, q] += i02 * r0 + i12 * r1 + i22 * r2
-        return forward(q, 0)
-
-    def keep(q, _):
-        for c, value in enumerate(misfit(q)):
-            resid[c, q] = value
-        return 0
+        forward(q, sweep + 1)
+        return sweep
 
     top = PAD + size_z
     arrived([(0, -1), (0, 1)])
     flat(pairs, pairs + own_pairs, stage_own)
     flat(PAD, top, forward)
-    elements(PAD, top - 1, False)
     flat(PAD + 1, top - 1, invert, sum_modes(PAD))
+    for sweep in range(SWEEPS + 1):
+        first, last = PAD + sweep, top - 1 - sweep
+        elements(sweep, first, last, False, False)
+        flat(first + 1, last, finish, sweep)
+
     arrived([side for side in SIDES if side[0] != 0])
     flat(0, pairs, stage_halo)
     flat(pairs + own_pairs, 2 * pairs + own_pairs, stage_halo)
     flat(1, PAD, forward)
     flat(top, planes, forward)
-    held = [[back[k, PAD, at] for at in tiles] for k in range(12)]
-    elements(1, PAD, False)
-    for k in range(12):
-        for at, value in zip(tiles, held[k]):
-            back[k, PAD, at] += value
-    elements(top - 1, planes - 1, True)
     flat(2, PAD + 1, invert, sum_modes(1))
     flat(top - 1, planes - 1, invert, sum_modes(top - 2))
-    flat(2, planes - 1, update)
-    for sweep in range(1, SWEEPS):
-        elements(sweep + 1, planes - 1 - sweep, False)
-        flat(sweep + 2, planes - 1 - sweep, update)
-    elements(PAD - 1, top + 1, False)
-    flat(PAD, top + 1, keep)
+    for sweep in range(SWEEPS + 1):
+        elements(sweep, 1 + sweep, PAD + sweep, False, True)
+        elements(sweep, top - 1 - sweep, planes - 1 - sweep, True, False)
+        flat(2 + sweep, PAD + sweep + 1, finish, sweep)
+        flat(top - 1 - sweep, planes - 1 - sweep, finish, sweep)
     for c in range(3):
         for z in range(size_z):
             smooth[c, z] = cur[c, PAD + z, 0:size_y]
@@ -567,8 +568,8 @@
             pltpu.VMEM((3, *block), F32),
             pltpu.VMEM(block, F32),
             pltpu.VMEM((6, *block), F32),
-            pltpu.VMEM((12, *block), F32),
-            pltpu.VMEM((12, *block), F32),
+            pltpu.VMEM((SWEEPS + 1, 12, *block), F32),
+            pltpu.VMEM((SWEEPS + 1, 12, *block), F32),
             pltpu.VMEM((3, *block), F32),
             pltpu.SemaphoreType.DMA((len(SIDES), 4)),
             pltpu.SemaphoreType.DMA((len(SIDES), 4)),

time: 19.5 us -> 18.2 us (0.933)
  Pallas kernels: 16.5 us -> 15.2 us
    pallas_call x1, Pallas kernels: 16.5 us -> 15.2 us  [on_device(): pl.pallas_call(functools.partial(kernel, unroll=UNROLL), out_shape=(jax.S...]
where the time goes in v3:
time: 18.2 us; the launch traced here: 18 us
  Pallas kernels  15.2 us (84%)
  local copies, waits for them, and re-layouts  2.22 us (12%)
  between operations  0.65 us (4%)
    pallas_call x1, Pallas kernels, on_device(): pl.pallas_call(functools.partial(kernel, unroll=UNROLL), out_shape=(jax.S...  15.2 us
    unnamed x4, local copies, waits for them, and re-layouts  2.22 us

profile of v3, /device:TPU:11, one launch (start us, length us, event | category | flops | bytes accessed | tf_op | source)
XLA Modules:
  0.0 18.0 jit_solution(6735220519131625658)
XLA Ops:
  0.6 15.2 %sweeps.1 = (f32[3,8,16,128]{3,2,1,0:T(8,128)}, f32[6,2,128]{2,1,0:T(2,128)}) custom-call(s32[8]{0:T(128)} %seg_z_hbm.1, s32[16]{0:T(128)} %seg_y_hbm.1, s32[1,128]{1,0:T(1,128)} %bitcast.1, f32[3,8,16,128]{3,2,1,0:T(8,128)} %field_hbm.1, f32[3,8,16,128]{3,2,1,0:T(8,128)} %load_hbm.1, f32[8,16,128]{2,1,0:T(8,128)} %mod_hbm.1), custom_call_target="tpu_custom_call" | custom-call | tf_op jit(solution)/shard_map/sweeps/pallas_call | solution.py:545
  15.8 0.0 copy-start
  15.8 1.6 %copy.10 = f32[3,8,16,128]{3,2,1,0:T(8,128)} copy(f32[3,8,16,128]{3,2,1,0:T(8,128)} %get-tuple-element.4) | data formatting | bytes 393216
  17.4 0.0 copy-done
  17.4 0.6 %copy.11 = f32[6,2,128]{2,1,0:T(2,128)} copy(f32[6,2,128]{2,1,0:T(2,128)S(1)} %copy-done) | data formatting | bytes 12288
Async XLA Ops:
  15.8 1.6 %copy-start = (f32[6,2,128]{2,1,0:T(2,128)S(1)}, f32[6,2,128]{2,1,0:T(2,128)}, u32[]{:S(2)}) copy-start(f32[6,2,128]{2,1,0:T(2,128)} %get-tuple-element.5) | copy-start | bytes 18436

commit v4 on v3

--- a/solution.py
+++ b/solution.py
@@ -14,10 +14,11 @@
 POISSON = 0.3
 LAME = POISSON / ((1.0 + POISSON) * (1.0 - 2.0 * POISSON))
 SHEAR = 0.5 / (1.0 + POISSON)
-SIDES = ((-1, 0), (1, 0), (0, -1), (0, 1), (-1, -1), (-1, 1), (1, -1), (1, 1))
+SIDES = ((0, -1), (0, 1), (-1, 0), (1, 0), (-1, -1), (1, 1), (-1, 1), (1, -1))
 UNROLL = 2
 MESH = pl.DeviceIdType.MESH
 F32 = jnp.float32
+BF16 = jnp.bfloat16
 
 
 def element_modes(lo, hi, e):
@@ -73,6 +74,22 @@
     for c in range(3):
         out[c][1][1][1] = e_last * diff(c, 1, 1)
     return out
+
+
+def corner_planes(dz, size_z):
+    held = []
+    for k in range(7):
+        low, high = REACH[k // 3]
+        if dz == 1:
+            held += [(k, size_z - low + i, PAD - low + i) for i in range(low)]
+        else:
+            held += [(k, i, PAD + size_z + i) for i in range(high)]
+    return held
+
+
+def two_parts(v):
+    high = v.astype(BF16)
+    return high, (v - high.astype(F32)).astype(BF16)
 
 
 def flat(first, last, body, carry=0):
@@ -97,8 +114,11 @@
     load,
     mod,
     own_sem,
+    result_sem,
     packed,
     tails,
+    corners,
+    corner_tails,
     halo,
     mark,
     marked,
@@ -121,7 +141,6 @@
     slabs, subs = lax.axis_size("slab"), lax.axis_size("sub")
     total_z, total_y = size_z * slabs, size_y * subs
     parts_z, parts_y, parts_x = size_z // 4, size_y // 4, width // 4
-    pairs = PAD // 2
     own_pairs = size_z // 2
 
     def present(dz, dy):
@@ -180,6 +199,19 @@
         return 0
 
     flat(0, own_pairs, pack)
+    for dz in (-1, 1):
+        held = corner_planes(dz, size_z)
+        for n in range(0, len(held), 2):
+            (ka, za, _), (kb, zb, _) = held[n], held[min(n + 1, len(held) - 1)]
+            a, b = unit(inputs, ka), unit(inputs, kb)
+            corners[0, (dz + 1) // 2, n // 2] = jnp.where(
+                first_half, a[za, 0:8], pltpu.roll(b[zb, 0:8], PAD, 0)
+            )
+            corners[1, (dz + 1) // 2, n // 2] = jnp.where(
+                first_half,
+                pltpu.roll(b[zb, size_y - 8 : size_y], PAD, 0),
+                a[za, size_y - 8 : size_y],
+            )
     mark[0] = jnp.full((8, width), seg_z[0].astype(F32))
     mark[1] = jnp.full((8, width), seg_y[0].astype(F32))
 
@@ -208,17 +240,12 @@
                     group.append((src.at[pl.ds(start, count)], halo.at[6, pl.ds(to, count)]))
         else:
             which = 0 if dy == -1 else 1
-            start, to, count = {
-                -1: (0, pairs + own_pairs, pairs),
-                0: (0, pairs, own_pairs),
-                1: (own_pairs - pairs, 0, pairs),
-            }[dz]
-            group.append(
-                (
-                    packed.at[which, :, pl.ds(start, count)],
-                    tails.at[which, :, pl.ds(to, count)],
-                )
-            )
+            if dz == 0:
+                group.append((packed.at[which], tails.at[which]))
+            else:
+                tall = pl.ds(0, (len(corner_planes(dz, size_z)) + 1) // 2)
+                at = (which, (dz + 1) // 2, tall)
+                group.append((corners.at[at], corner_tails.at[at]))
         if (dz, dy) == (-1, 0):
             group.append((mark.at[0], marked.at[0]))
         if (dz, dy) == (0, -1):
@@ -253,11 +280,17 @@
     part = lax.rem(lax.broadcasted_iota(jnp.int32, square, 0), parts_x)
     weight_x = jnp.where(seg_x[...] == part, 1.0, 0.0)
     place_x = 0.5 * (lax.broadcasted_iota(jnp.int32, square, 1) - 4 * part - 2).astype(F32)
-    count = jnp.sum(weight_x, axis=1, keepdims=True)
-    centre = jnp.sum(weight_x * place_x, axis=1, keepdims=True) / count
-    weight_x = weight_x * lax.rsqrt(count)
-    weights_x[0 : square[0]] = weight_x
-    weights_x[square[0] : 2 * square[0]] = weight_x * (place_x - centre)
+    weight_x = jnp.concatenate([weight_x, weight_x * place_x], axis=0).astype(BF16)
+    weights_x[:, 0:width] = weight_x
+    weights_x[:, width : 2 * width] = weight_x
+    alone = lax.dot_general(
+        jnp.ones((16, width), BF16),
+        weight_x,
+        (((1,), (1,)), ((), ())),
+        preferred_element_type=F32,
+    )
+    spread = square[0]
+    count_x, moment_x = alone[0:1, 0:spread], alone[0:1, spread : 2 * spread]
 
     first_z = slab * size_z - PAD
     row = lax.broadcasted_iota(jnp.int32, (rows, width), 0)
@@ -285,36 +318,37 @@
     def upper(v):
         return pltpu.roll(v, 1, 0)
 
-    def stage(i, refs, shift):
+    def place(k, q, main, above, below, odd):
+        if odd:
+            end = pltpu.roll(jnp.where(first_half, below, above), PAD, 0)
+        else:
+            end = jnp.where(first_half, above, below)
+        value = jnp.concatenate([main, end], axis=0)
+        glob_z = q + first_z
+        if k < 6:
+            keep = rows_in & (glob_z >= 0) & (glob_z < total_z)
+            value = jnp.where(keep, value, 0.0)
+            if k < 3:
+                cur[k, q] = value
+            else:
+                right_side[k - 3, q] = value
+        else:
+            keep = elements_in & (glob_z >= 0) & (glob_z < total_z - 1)
+            emod[q] = jnp.where(keep, value, 0.0)
+
+    def stage_own(i, _):
         for k in range(7):
-            src = unit(refs, k) if shift else halo.at[k]
-            above, below = tails[0, k, i], tails[1, k, i]
-            ends = (
-                jnp.where(first_half, above, below),
-                pltpu.roll(jnp.where(first_half, below, above), PAD, 0),
-            )
+            src = unit(inputs, k)
             for odd in range(2):
-                q = 2 * i + odd
-                glob_z = q + first_z
-                value = jnp.concatenate([src[q - shift], ends[odd]], axis=0)
-                if k < 6:
-                    keep = rows_in & (glob_z >= 0) & (glob_z < total_z)
-                    value = jnp.where(keep, value, 0.0)
-                    if k < 3:
-                        cur[k, q] = value
-                    else:
-                        right_side[k - 3, q] = value
-                else:
-                    keep = elements_in & (glob_z >= 0) & (glob_z < total_z - 1)
-                    emod[q] = jnp.where(keep, value, 0.0)
-
-    def stage_own(i, _):
-        stage(i, inputs, PAD)
+                z = 2 * i + odd
+                place(k, z + PAD, src[z], tails[0, k, i], tails[1, k, i], odd)
         return 0
 
-    def stage_halo(i, _):
-        stage(i, None, 0)
-        return 0
+    def stage_halo(dz):
+        side = (dz + 1) // 2
+        for n, (k, _, q) in enumerate(corner_planes(dz, size_z)):
+            above, below = corner_tails[0, side, n // 2], corner_tails[1, side, n // 2]
+            place(k, q, halo[k, q], above, below, n % 2)
 
     def sum_modes(q):
         e = emod[q]
@@ -425,7 +459,7 @@
 
     top = PAD + size_z
     arrived([(0, -1), (0, 1)])
-    flat(pairs, pairs + own_pairs, stage_own)
+    flat(0, own_pairs, stage_own)
     flat(PAD, top, forward)
     flat(PAD + 1, top - 1, invert, sum_modes(PAD))
     for sweep in range(SWEEPS + 1):
@@ -434,24 +468,26 @@
         flat(first + 1, last, finish, sweep)
 
     arrived([side for side in SIDES if side[0] != 0])
-    flat(0, pairs, stage_halo)
-    flat(pairs + own_pairs, 2 * pairs + own_pairs, stage_halo)
+    stage_halo(1)
+    stage_halo(-1)
     flat(1, PAD, forward)
     flat(top, planes, forward)
     flat(2, PAD + 1, invert, sum_modes(1))
     flat(top - 1, planes - 1, invert, sum_modes(top - 2))
+    result = pltpu.make_async_copy(
+        cur.at[:, pl.ds(PAD, size_z), pl.ds(0, size_y)], smooth, result_sem
+    )
     for sweep in range(SWEEPS + 1):
+        if sweep == SWEEPS:
+            result.start()
         elements(sweep, 1 + sweep, PAD + sweep, False, True)
         elements(sweep, top - 1 - sweep, planes - 1 - sweep, True, False)
         flat(2 + sweep, PAD + sweep + 1, finish, sweep)
         flat(top - 1 - sweep, planes - 1 - sweep, finish, sweep)
-    for c in range(3):
-        for z in range(size_z):
-            smooth[c, z] = cur[c, PAD + z, 0:size_y]
-
     seg_after_z = marked[0, 0:1, :]
     seg_after_y = marked[1, 0:1, :]
     maps = []
+    along_z = []
     for k in range(parts_z):
         want = slab * parts_z + k
         weights = []
@@ -459,15 +495,10 @@
         for z in range(size_z):
             weights.append(jnp.where(seg_z[z] == want, 1.0, 0.0).astype(F32))
             places.append(0.5 * (slab * size_z + z - 4 * want - 2).astype(F32))
-        count = sum(weights)
-        moment = sum(w * p for w, p in zip(weights, places))
         last = jnp.where((seg_after_z == want.astype(F32)) & (slab < slabs - 1), 1.0, 0.0)
-        place = 0.5 * ((slab + 1) * size_z - 4 * want - 2).astype(F32)
         weights.append(last)
-        places.append(place)
-        count = count + last
-        centre = (moment + last * place) / count
-        scale = lax.rsqrt(count)
+        places.append(0.5 * ((slab + 1) * size_z - 4 * want - 2).astype(F32))
+        along_z.append((sum(weights), sum(w * p for w, p in zip(weights, places))))
         sums = [jnp.zeros((rows, width), F32) for _ in range(3)]
         turns = [jnp.zeros((rows, width), F32) for _ in range(2)]
         for z in range(size_z + 1):
@@ -476,8 +507,7 @@
                 sums[c] = sums[c] + part
                 if c < 2:
                     turns[c] = turns[c] + places[z] * part
-        maps += [scale * s for s in sums]
-        maps += [scale * (turns[c] - centre * sums[c]) for c in range(2)]
+        maps += sums + turns
 
     lane = lax.broadcasted_iota(jnp.int32, (2 * parts_y, rows), 1)
     part = lax.broadcasted_iota(jnp.int32, (2 * parts_y, rows), 0)
@@ -490,42 +520,45 @@
     hit = (lane == size_y) & (after == part.astype(F32)) & (sub < subs - 1)
     weight_y = jnp.where((segments == part) | hit, 1.0, 0.0)
     place_y = 0.5 * (lane + sub * size_y - 4 * part - 2).astype(F32)
-    count = jnp.sum(weight_y, axis=1, keepdims=True)
-    centre = jnp.sum(weight_y * place_y, axis=1, keepdims=True) / count
-    weight_y = weight_y * lax.rsqrt(count) * jnp.where(turned, place_y - centre, 1.0)
-
-    wide = jnp.concatenate(maps, axis=1)
-    by_y = jnp.dot(
-        weight_y, wide, precision=lax.Precision.HIGHEST, preferred_element_type=F32
-    )
+    weight_y = weight_y * jnp.where(turned, place_y, 1.0)
+    along_y = jnp.sum(weight_y, axis=1, keepdims=True)
+
+    high, low = two_parts(jnp.concatenate(maps, axis=1))
+    weight_y = weight_y.astype(BF16)
+    by_y = jnp.dot(weight_y, high, preferred_element_type=F32)
+    by_y = by_y + jnp.dot(weight_y, low, preferred_element_type=F32)
     tall = jnp.concatenate(
         [by_y[:, width * k : width * (k + 1)] for k in range(len(maps))], axis=0
     )
     by_x = lax.dot_general(
-        tall,
+        jnp.concatenate(two_parts(tall), axis=1),
         weights_x[...],
         (((1,), (1,)), ((), ())),
-        precision=lax.Precision.HIGHEST,
         preferred_element_type=F32,
     )
-    spread = parts_y * parts_x
     pick = lax.broadcasted_iota(jnp.int32, (parts_y, spread), 0) == (
         lax.broadcasted_iota(jnp.int32, (parts_y, spread), 1) // parts_x
     )
 
+    def picked(block):
+        return jnp.sum(jnp.where(pick, block, 0.0), axis=0, keepdims=True)
+
     def chosen(k, turn_y, turn_x):
         start = (2 * k + turn_y) * parts_y
-        block = by_x[start : start + parts_y, turn_x * spread : (turn_x + 1) * spread]
-        return jnp.sum(jnp.where(pick, block, 0.0), axis=0, keepdims=True)
-
+        return picked(by_x[start : start + parts_y, turn_x * spread : (turn_x + 1) * spread])
+
+    count_y, moment_y = picked(along_y[0:parts_y]), picked(along_y[parts_y : 2 * parts_y])
     for k in range(parts_z):
         b = 5 * k
-        values = [chosen(b, 0, 0), chosen(b + 1, 0, 0), chosen(b + 2, 0, 0)]
-        values.append(chosen(b + 2, 1, 0) - chosen(b + 4, 0, 0))
-        values.append(chosen(b + 3, 0, 0) - chosen(b + 2, 0, 1))
-        values.append(chosen(b + 1, 0, 1) - chosen(b, 1, 0))
-        for c in range(6):
-            coarse[c, k : k + 1, :] = values[c]
+        count_z, moment_z = along_z[k]
+        centre_x, centre_y, centre_z = moment_x / count_x, moment_y / count_y, moment_z / count_z
+        scale = lax.rsqrt(count_x * count_y * count_z)
+        s0, s1, s2 = chosen(b, 0, 0), chosen(b + 1, 0, 0), chosen(b + 2, 0, 0)
+        t0 = chosen(b + 2, 1, 0) - chosen(b + 4, 0, 0) - (centre_y * s2 - centre_z * s1)
+        t1 = chosen(b + 3, 0, 0) - chosen(b + 2, 0, 1) - (centre_z * s0 - centre_x * s2)
+        t2 = chosen(b + 1, 0, 1) - chosen(b, 1, 0) - (centre_x * s1 - centre_y * s0)
+        for c, value in enumerate((s0, s1, s2, t0, t1, t2)):
+            coarse[c, k : k + 1, :] = value * scale
 
     for dz, dy in SIDES:
 
@@ -533,6 +566,8 @@
         def _():
             for copy in copies[dz, dy]:
                 copy.wait_send()
+
+    result.wait()
 
 
 def on_device(field_init, load, modulus, seg_z, seg_y, seg_x):
@@ -542,6 +577,7 @@
     hbm = pl.BlockSpec(memory_space=pltpu.HBM)
     vmem = pl.BlockSpec(memory_space=pltpu.VMEM)
     block = (planes, rows, width)
+    corner_tiles = max((len(corner_planes(dz, size_z)) + 1) // 2 for dz in (-1, 1))
     smooth, coarse = pl.pallas_call(
         functools.partial(kernel, unroll=UNROLL),
         out_shape=(
@@ -549,7 +585,7 @@
             jax.ShapeDtypeStruct((6, size_z // 4, size_y * width // 16), F32),
         ),
         in_specs=[hbm] * 6,
-        out_specs=(vmem, vmem),
+        out_specs=(hbm, vmem),
         scratch_shapes=[
             pltpu.SMEM(seg_z.shape, jnp.int32),
             pltpu.SMEM(seg_y.shape, jnp.int32),
@@ -558,12 +594,15 @@
             pltpu.VMEM(load.shape, F32),
             pltpu.VMEM(modulus.shape, F32),
             pltpu.SemaphoreType.DMA((6,)),
+            pltpu.SemaphoreType.DMA,
             pltpu.VMEM((2, 7, size_z // 2, 8, width), F32),
-            pltpu.VMEM((2, 7, planes // 2, 8, width), F32),
+            pltpu.VMEM((2, 7, size_z // 2, 8, width), F32),
+            pltpu.VMEM((2, 2, corner_tiles, 8, width), F32),
+            pltpu.VMEM((2, 2, corner_tiles, 8, width), F32),
             pltpu.VMEM((7, planes, size_y, width), F32),
             pltpu.VMEM((2, 8, width), F32),
             pltpu.VMEM((2, 8, width), F32),
-            pltpu.VMEM((size_y * width // 8, width), F32),
+            pltpu.VMEM((size_y * width // 8, 2 * width), BF16),
             pltpu.VMEM((3, *block), F32),
             pltpu.VMEM((3, *block), F32),
             pltpu.VMEM(block, F32),

time: 18.2 us -> 17.4 us (0.956)
  Pallas kernels: 15.2 us -> 14.4 us
    pallas_call x1, Pallas kernels: 15.2 us -> 14.4 us  [on_device(): pl.pallas_call(functools.partial(kernel, unroll=UNROLL), out_shape=(jax.S...]
where the time goes in v4:
time: 17.4 us; the launch traced here: 17.2 us
  Pallas kernels  14.4 us (83%)
  local copies, waits for them, and re-layouts  2.22 us (13%)
  between operations  0.65 us (4%)
    pallas_call x1, Pallas kernels, on_device(): pl.pallas_call(functools.partial(kernel, unroll=UNROLL), out_shape=(jax.S...  14.4 us
    unnamed x4, local copies, waits for them, and re-layouts  2.22 us

profile of v4, /device:TPU:11, one launch (start us, length us, event | category | flops | bytes accessed | tf_op | source)
XLA Modules:
  0.0 17.2 jit_solution(10152243448889406148)
XLA Ops:
  0.6 14.4 %sweeps.1 = (f32[3,8,16,128]{3,2,1,0:T(8,128)}, f32[6,2,128]{2,1,0:T(2,128)}) custom-call(s32[8]{0:T(128)} %seg_z_hbm.1, s32[16]{0:T(128)} %seg_y_hbm.1, s32[1,128]{1,0:T(1,128)} %bitcast.1, f32[3,8,16,128]{3,2,1,0:T(8,128)} %field_hbm.1, f32[3,8,16,128]{3,2,1,0:T(8,128)} %load_hbm.1, f32[8,16,128]{2,1,0:T(8,128)} %mod_hbm.1), custom_call_target="tpu_custom_call" | custom-call | tf_op jit(solution)/shard_map/sweeps/pallas_call | solution.py:581
  15.0 0.0 copy-start
  15.0 1.6 %copy.10 = f32[3,8,16,128]{3,2,1,0:T(8,128)} copy(f32[3,8,16,128]{3,2,1,0:T(8,128)} %get-tuple-element.4) | data formatting | bytes 393216
  16.6 0.0 copy-done
  16.6 0.6 %copy.11 = f32[6,2,128]{2,1,0:T(2,128)} copy(f32[6,2,128]{2,1,0:T(2,128)S(1)} %copy-done) | data formatting | bytes 12288
Async XLA Ops:
  15.0 1.6 %copy-start = (f32[6,2,128]{2,1,0:T(2,128)S(1)}, f32[6,2,128]{2,1,0:T(2,128)}, u32[]{:S(2)}) copy-start(f32[6,2,128]{2,1,0:T(2,128)} %get-tuple-element.5) | copy-start | bytes 18436

commit v5 on v4

--- a/solution.py
+++ b/solution.py
@@ -467,23 +467,39 @@
         elements(sweep, first, last, False, False)
         flat(first + 1, last, finish, sweep)
 
-    arrived([side for side in SIDES if side[0] != 0])
-    stage_halo(1)
-    stage_halo(-1)
-    flat(1, PAD, forward)
-    flat(top, planes, forward)
-    flat(2, PAD + 1, invert, sum_modes(1))
-    flat(top - 1, planes - 1, invert, sum_modes(top - 2))
     result = pltpu.make_async_copy(
         cur.at[:, pl.ds(PAD, size_z), pl.ds(0, size_y)], smooth, result_sem
     )
-    for sweep in range(SWEEPS + 1):
-        if sweep == SWEEPS:
-            result.start()
-        elements(sweep, 1 + sweep, PAD + sweep, False, True)
-        elements(sweep, top - 1 - sweep, planes - 1 - sweep, True, False)
-        flat(2 + sweep, PAD + sweep + 1, finish, sweep)
-        flat(top - 1 - sweep, planes - 1 - sweep, finish, sweep)
+
+    def group(dz, final):
+        arrived([side for side in SIDES if side[0] == dz])
+        stage_halo(dz)
+        if dz == 1:
+            flat(1, PAD, forward)
+            flat(2, PAD + 1, invert, sum_modes(1))
+        else:
+            flat(top, planes, forward)
+            flat(top - 1, planes - 1, invert, sum_modes(top - 2))
+        for sweep in range(SWEEPS + 1):
+            if final and sweep == SWEEPS:
+                result.start()
+            if dz == 1:
+                elements(sweep, 1 + sweep, PAD + sweep, False, True)
+                flat(2 + sweep, PAD + sweep + 1, finish, sweep)
+            else:
+                elements(sweep, top - 1 - sweep, planes - 1 - sweep, True, False)
+                flat(top - 1 - sweep, planes - 1 - sweep, finish, sweep)
+
+    @pl.when(lax.rem(slab, 2) == 1)
+    def _():
+        group(1, False)
+        group(-1, True)
+
+    @pl.when(lax.rem(slab, 2) == 0)
+    def _():
+        group(-1, False)
+        group(1, True)
+
     seg_after_z = marked[0, 0:1, :]
     seg_after_y = marked[1, 0:1, :]
     maps = []

time: 17.4 us -> 17.3 us (level)
  the two profiles are of different devices: /device:TPU:11 before, /device:TPU:0 now
where the time goes in v5:
time: 17.3 us; the launch traced here: 17.2 us
  Pallas kernels  14.3 us (83%)
  local copies, waits for them, and re-layouts  2.22 us (13%)
  between operations  0.65 us (4%)
    pallas_call x1, Pallas kernels, on_device(): pl.pallas_call(functools.partial(kernel, unroll=UNROLL), out_shape=(jax.S...  14.3 us
    unnamed x4, local copies, waits for them, and re-layouts  2.22 us

profile of v5, /device:TPU:0, one launch (start us, length us, event | category | flops | bytes accessed | tf_op | source)
XLA Modules:
  0.0 17.2 jit_solution(17385245644490566923)
XLA Ops:
  0.6 14.3 %sweeps.1 = (f32[3,8,16,128]{3,2,1,0:T(8,128)}, f32[6,2,128]{2,1,0:T(2,128)}) custom-call(s32[8]{0:T(128)} %seg_z_hbm.1, s32[16]{0:T(128)} %seg_y_hbm.1, s32[1,128]{1,0:T(1,128)} %bitcast.1, f32[3,8,16,128]{3,2,1,0:T(8,128)} %field_hbm.1, f32[3,8,16,128]{3,2,1,0:T(8,128)} %load_hbm.1, f32[8,16,128]{2,1,0:T(8,128)} %mod_hbm.1), custom_call_target="tpu_custom_call" | custom-call | tf_op jit(solution)/shard_map/sweeps/pallas_call | solution.py:597
  15.0 0.0 copy-start
  15.0 1.6 %copy.10 = f32[3,8,16,128]{3,2,1,0:T(8,128)} copy(f32[3,8,16,128]{3,2,1,0:T(8,128)} %get-tuple-element.4) | data formatting | bytes 393216
  16.6 0.0 copy-done
  16.6 0.6 %copy.11 = f32[6,2,128]{2,1,0:T(2,128)} copy(f32[6,2,128]{2,1,0:T(2,128)S(1)} %copy-done) | data formatting | bytes 12288
Async XLA Ops:
  15.0 1.6 %copy-start = (f32[6,2,128]{2,1,0:T(2,128)S(1)}, f32[6,2,128]{2,1,0:T(2,128)}, u32[]{:S(2)}) copy-start(f32[6,2,128]{2,1,0:T(2,128)} %get-tuple-element.5) | copy-start | bytes 18436

commit v6 on v4

--- a/solution.py
+++ b/solution.py
@@ -1,5 +1,3 @@
-import functools
-
 import jax
 import jax.numpy as jnp
 from jax import lax
@@ -15,7 +13,6 @@
 LAME = POISSON / ((1.0 + POISSON) * (1.0 - 2.0 * POISSON))
 SHEAR = 0.5 / (1.0 + POISSON)
 SIDES = ((0, -1), (0, 1), (-1, 0), (1, 0), (-1, -1), (1, 1), (-1, 1), (1, -1))
-UNROLL = 2
 MESH = pl.DeviceIdType.MESH
 F32 = jnp.float32
 BF16 = jnp.bfloat16
@@ -113,6 +110,7 @@
     field,
     load,
     mod,
+    correction,
     own_sem,
     result_sem,
     packed,
@@ -132,8 +130,6 @@
     resid,
     send_sem,
     recv_sem,
-    *,
-    unroll,
 ):
     size_z, size_y, width = smooth.shape[1:]
     planes, rows = cur.shape[1], cur.shape[2]
@@ -424,7 +420,7 @@
                 carry = tuple(back[sweep, k, first, at] for k in range(12))
             else:
                 carry = (jnp.zeros((8, width), F32),) * 12
-            carry = lax.fori_loop(first, last, element, carry, unroll=unroll)
+            carry = flat(first, last, element, carry)
             for k in range(12):
                 if add:
                     back[sweep, k, last, at] += carry[k]
@@ -475,10 +471,13 @@
     flat(2, PAD + 1, invert, sum_modes(1))
     flat(top - 1, planes - 1, invert, sum_modes(top - 2))
     result = pltpu.make_async_copy(
-        cur.at[:, pl.ds(PAD, size_z), pl.ds(0, size_y)], smooth, result_sem
+        correction, smooth, result_sem
     )
     for sweep in range(SWEEPS + 1):
         if sweep == SWEEPS:
+            for c in range(3):
+                for z in range(size_z):
+                    correction[c, z] = cur[c, PAD + z, 0:size_y] - field[c, z]
             result.start()
         elements(sweep, 1 + sweep, PAD + sweep, False, True)
         elements(sweep, top - 1 - sweep, planes - 1 - sweep, True, False)
@@ -579,7 +578,7 @@
     block = (planes, rows, width)
     corner_tiles = max((len(corner_planes(dz, size_z)) + 1) // 2 for dz in (-1, 1))
     smooth, coarse = pl.pallas_call(
-        functools.partial(kernel, unroll=UNROLL),
+        kernel,
         out_shape=(
             jax.ShapeDtypeStruct((3, size_z, size_y, width), F32),
             jax.ShapeDtypeStruct((6, size_z // 4, size_y * width // 16), F32),
@@ -593,6 +592,7 @@
             pltpu.VMEM(field_init.shape, F32),
             pltpu.VMEM(load.shape, F32),
             pltpu.VMEM(modulus.shape, F32),
+            pltpu.VMEM(field_init.shape, F32),
             pltpu.SemaphoreType.DMA((6,)),
             pltpu.SemaphoreType.DMA,
             pltpu.VMEM((2, 7, size_z // 2, 8, width), F32),
@@ -618,7 +618,7 @@
         ),
         name="sweeps",
     )(seg_z, seg_y, seg_x.reshape(1, width), field_init, load, modulus)
-    return smooth, coarse
+    return field_init + smooth, coarse
 
 
 def solution(mesh):

time: 17.4 us -> 17.9 us (1.029)
  other arithmetic: 0 us -> 1.73 us
  local copies, waits for them, and re-layouts: 2.22 us -> 0.6 us
  Pallas kernels: 14.4 us -> 14.7 us
    add x0 -> x1, other arithmetic: none -> 1.73 us  [on_device(): return (field_init + smooth, coarse)]
    unnamed x4 -> x3, local copies, waits for them, and re-layouts: 2.22 us -> 0.6 us
    pallas_call x1, Pallas kernels: 14.4 us -> 14.7 us  [on_device(): pl.pallas_call(kernel, out_shape=(jax.ShapeDtypeStruct((3, size_z, size_y...]
where the time goes in v6:
time: 17.9 us; the launch traced here: 17.7 us
  Pallas kernels  14.7 us (82%)
  other arithmetic  1.73 us (10%)
  between operations  0.65 us (4%)
  local copies, waits for them, and re-layouts  0.6 us (3%)
    pallas_call x1, Pallas kernels, on_device(): pl.pallas_call(kernel, out_shape=(jax.ShapeDtypeStruct((3, size_z, size_y...  14.7 us
    add x1, other arithmetic, on_device(): return (field_init + smooth, coarse)  1.73 us
    unnamed x3, local copies, waits for them, and re-layouts  0.6 us

profile of v6, /device:TPU:11, one launch (start us, length us, event | category | flops | bytes accessed | tf_op | source)
XLA Modules:
  0.0 17.7 jit_solution(8838312659784578716)
XLA Ops:
  0.6 14.7 %sweeps.1 = (f32[3,8,16,128]{3,2,1,0:T(8,128)}, f32[6,2,128]{2,1,0:T(2,128)}) custom-call(s32[8]{0:T(128)} %seg_z_hbm.1, s32[16]{0:T(128)} %seg_y_hbm.1, s32[1,128]{1,0:T(1,128)} %bitcast.1, f32[3,8,16,128]{3,2,1,0:T(8,128)} %field_hbm.1, f32[3,8,16,128]{3,2,1,0:T(8,128)} %load_hbm.1, f32[8,16,128]{2,1,0:T(8,128)} %mod_hbm.1), custom_call_target="tpu_custom_call" | custom-call | tf_op jit(solution)/shard_map/sweeps/pallas_call | solution.py:580
  15.4 0.0 copy-start
  15.4 1.7 %add.3 = f32[3,8,16,128]{3,2,1,0:T(8,128)} add(f32[3,8,16,128]{3,2,1,0:T(8,128)} %field_hbm.1, f32[3,8,16,128]{3,2,1,0:T(8,128)} %get-tuple-element.4) | non-fusion elementwise | flops 49152 | bytes 589824 | tf_op jit(solution)/shard_map/add | solution.py:621
  17.1 0.0 copy-done
  17.1 0.6 %copy.9 = f32[6,2,128]{2,1,0:T(2,128)} copy(f32[6,2,128]{2,1,0:T(2,128)S(1)} %copy-done) | data formatting | bytes 12288
Async XLA Ops:
  15.4 1.7 %copy-start = (f32[6,2,128]{2,1,0:T(2,128)S(1)}, f32[6,2,128]{2,1,0:T(2,128)}, u32[]{:S(2)}) copy-start(f32[6,2,128]{2,1,0:T(2,128)} %get-tuple-element.9) | copy-start | bytes 18436

commit v7 on v4

--- a/solution.py
+++ b/solution.py
@@ -15,7 +15,7 @@
 LAME = POISSON / ((1.0 + POISSON) * (1.0 - 2.0 * POISSON))
 SHEAR = 0.5 / (1.0 + POISSON)
 SIDES = ((0, -1), (0, 1), (-1, 0), (1, 0), (-1, -1), (1, 1), (-1, 1), (1, -1))
-UNROLL = 2
+UNROLL = 1
 MESH = pl.DeviceIdType.MESH
 F32 = jnp.float32
 BF16 = jnp.bfloat16

time: 17.4 us -> 17.6 us (1.011)
  Pallas kernels: 14.4 us -> 14.6 us
    pallas_call x1, Pallas kernels: 14.4 us -> 14.6 us  [on_device(): pl.pallas_call(functools.partial(kernel, unroll=UNROLL), out_shape=(jax.S...]
where the time goes in v7:
time: 17.6 us; the launch traced here: 17.5 us
  Pallas kernels  14.6 us (83%)
  local copies, waits for them, and re-layouts  2.22 us (13%)
  between operations  0.65 us (4%)
    pallas_call x1, Pallas kernels, on_device(): pl.pallas_call(functools.partial(kernel, unroll=UNROLL), out_shape=(jax.S...  14.6 us
    unnamed x4, local copies, waits for them, and re-layouts  2.22 us

profile of v7, /device:TPU:11, one launch (start us, length us, event | category | flops | bytes accessed | tf_op | source)
XLA Modules:
  0.0 17.5 jit_solution(7932430651911655817)
XLA Ops:
  0.6 14.6 %sweeps.1 = (f32[3,8,16,128]{3,2,1,0:T(8,128)}, f32[6,2,128]{2,1,0:T(2,128)}) custom-call(s32[8]{0:T(128)} %seg_z_hbm.1, s32[16]{0:T(128)} %seg_y_hbm.1, s32[1,128]{1,0:T(1,128)} %bitcast.1, f32[3,8,16,128]{3,2,1,0:T(8,128)} %field_hbm.1, f32[3,8,16,128]{3,2,1,0:T(8,128)} %load_hbm.1, f32[8,16,128]{2,1,0:T(8,128)} %mod_hbm.1), custom_call_target="tpu_custom_call" | custom-call | tf_op jit(solution)/shard_map/sweeps/pallas_call | solution.py:581
  15.3 0.0 copy-start
  15.3 1.6 %copy.10 = f32[3,8,16,128]{3,2,1,0:T(8,128)} copy(f32[3,8,16,128]{3,2,1,0:T(8,128)} %get-tuple-element.4) | data formatting | bytes 393216
  16.9 0.0 copy-done
  16.9 0.6 %copy.11 = f32[6,2,128]{2,1,0:T(2,128)} copy(f32[6,2,128]{2,1,0:T(2,128)S(1)} %copy-done) | data formatting | bytes 12288
Async XLA Ops:
  15.3 1.6 %copy-start = (f32[6,2,128]{2,1,0:T(2,128)S(1)}, f32[6,2,128]{2,1,0:T(2,128)}, u32[]{:S(2)}) copy-start(f32[6,2,128]{2,1,0:T(2,128)} %get-tuple-element.5) | copy-start | bytes 18436
